TPU v7x, 256 devices: a whole 4x4x8 slice. The times are simulated.
256 devices in a mesh: dcn: 2 (over x_lo), dp: 16 (over x_hi, y, core), tp: 8 (over z).
Axes of the slice: x: 4 (x_hi: 2, x_lo: 2; x = x_hi * 2 + x_lo), y: 4, z: 8, core: 2. Of those that a mesh axis runs over, the one named last changes fastest.
Arguments:
- tokens: bfloat16 [4096, 18432], P(('dcn', 'dp', 'tp')), may hold values from -24 to 24
- upstream: bfloat16 [4096, 18432], P(('dcn', 'dp', 'tp')), may hold values from -5 to 5
- w_in: bfloat16 [18432, 1024], P(None, 'tp'), may hold values from -0.046875 to 0.046875
- w_out: bfloat16 [1024, 18432], P('tp'), may hold values from -0.1875 to 0.1875
Outputs:
- tokens_grad: float32 [4096, 18432], P(('dcn', 'dp', 'tp'))
- in_grad: float32 [18432, 1024], P(('dcn', 'dp'), 'tp')
- out_grad: float32 [1024, 18432], P('tp', ('dcn', 'dp'))
All inputs are finite; a program needn't handle non-finite values.
Results may differ from a plain program's by a relative error of at most 0.0029.
Values may be sent and summed in bfloat16 or wider, within the bound.
A program may use at most 128 MiB of HBM per device.

v0:
```python
import jax
import jax.numpy as jnp
from jax import lax
from jax.sharding import PartitionSpec as P


def per_device(tokens, upstream, w_in, w_out):
    seq_rows, seq_grad = (
        lax.all_gather(tokens, "tp", axis=0, tiled=True),
        lax.all_gather(upstream, "tp", axis=0, tiled=True),
    )
    pre = jnp.dot(seq_rows, w_in, preferred_element_type=jnp.float32)
    positive = jnp.maximum(pre, 0.0)
    act = (positive * positive).astype(jnp.bfloat16)
    out_grad = lax.dot_general(
        act, seq_grad, (((0,), (0,)), ((), ())), preferred_element_type=jnp.float32
    )
    act_grad = lax.dot_general(
        seq_grad, w_out, (((1,), (1,)), ((), ())), preferred_element_type=jnp.float32
    )
    pre_grad = (act_grad * 2.0 * positive).astype(jnp.bfloat16)
    in_grad = lax.dot_general(
        seq_rows, pre_grad, (((0,), (0,)), ((), ())), preferred_element_type=jnp.float32
    )
    tokens_grad = lax.psum_scatter(
        lax.dot_general(
            pre_grad, w_in, (((1,), (1,)), ((), ())), preferred_element_type=jnp.float32
        ),
        "tp",
        scatter_dimension=0,
        tiled=True,
    )
    in_share, out_share = (
        lax.psum_scatter(in_grad, ("dcn", "dp"), scatter_dimension=0, tiled=True),
        lax.psum_scatter(out_grad, ("dcn", "dp"), scatter_dimension=1, tiled=True),
    )
    return (tokens_grad, in_share, out_share)


def solution(mesh):
    placed = (
        P(("dcn", "dp", "tp"), None),
        P(("dcn", "dp", "tp"), None),
        P(None, "tp"),
        P("tp", None),
    )
    return jax.shard_map(
        per_device,
        mesh=mesh,
        in_specs=placed,
        out_specs=(P(("dcn", "dp", "tp"), None), P(("dcn", "dp"), "tp"), P("tp", ("dcn", "dp"))),
        check_vma=False,
    )
```

profile of v0, /device:TPU:1, one launch (start us, length us, event | category | flops | bytes accessed | tf_op | source)
XLA Modules:
  0.0 560.5 jit_solution(3335883193395913392)
XLA Ops:
  7.2 0.0 all-gather.5.cloned.1.call-start
  7.2 0.7 all-gather.5.cloned.1.call-update
  7.9 0.0 all-gather.3.cloned.1.call-start
  7.9 0.7 all-gather.3.cloned.1.call-update
  8.6 0.0 reduce-scatter.8.cloned.1.call-start
  8.7 64.7 %all-gather.5.cloned.1.call-done = bf16[128,18432]{1,0:T(8,128)(2,1)} async-done(((bf16[16,18432]{1,0:T(8,128)(2,1)}), bf16[128,18432]{1,0:T(8,128)(2,1)}) %all-gather.5.cloned.1.call-update) | async-done | bytes 4718608 | tf_op jit(solution)/shard_map/all_gather | solution.py:9
  73.4 5.2 convolution_maximum_fusion
  78.5 55.0 %all-gather.3.cloned.1.call-done = bf16[128,18432]{1,0:T(8,128)(2,1)} async-done(((bf16[16,18432]{1,0:T(8,128)(2,1)}), bf16[128,18432]{1,0:T(8,128)(2,1)}) %all-gather.3.cloned.1.call-update) | async-done | bytes 4718608 | tf_op jit(solution)/shard_map/all_gather | solution.py:10
  133.5 7.9 %fusion.2 = f32[128,18432]{0,1:T(8,128)} fusion(bf16[128,18432]{1,0:T(8,128)(2,1)} %all-gather.3.cloned.1.call-done, f32[128,128]{1,0:T(8,128)S(1)} %convolution_maximum_fusion), kind=kOutput, calls=%fused_computation.6 | convolution fusion | flops 604012544 | bytes 14221312 | tf_op jit(solution)/shard_map/dot_general | solution.py:15
  141.4 0.0 reduce-scatter.8.cloned.1.call-update
  141.5 0.0 reduce-scatter.10.cloned.1.call-start
  141.5 5.2 fusion.1
  146.7 7.5 %convolution_bitcast_fusion = f32[18432,128]{0,1:T(8,128)} fusion(bf16[128,128]{1,0:T(8,128)(2,1)S(1)} %fusion.1, bf16[128,18432]{1,0:T(8,128)(2,1)} %all-gather.5.cloned.1.call-done), kind=kOutput, calls=%fused_computation | convolution fusion | flops 603979776 | bytes 14188544 | tf_op jit(solution)/shard_map/dot_general | solution.py:22
  154.1 9.7 %copy.9 = f32[18432,128]{1,0:T(8,128)} copy(f32[18432,128]{0,1:T(8,128)} %convolution_bitcast_fusion) | data formatting | bytes 18874368
  163.8 0.0 reduce-scatter.10.cloned.1.call-update
  163.8 0.0 reduce-scatter.6.cloned.1.call-start
  163.9 7.5 %fusion.3 = f32[128,18432]{1,0:T(8,128)} fusion(bf16[128,128]{1,0:T(8,128)(2,1)S(1)} %fusion.1, bf16[18432,128]{1,0:T(8,128)(2,1)} %param.6), kind=kOutput, calls=%fused_computation.7 | convolution fusion | flops 603979776 | bytes 14188544 | tf_op jit(solution)/shard_map/dot_general | solution.py:26
  171.3 0.0 reduce-scatter.6.cloned.1.call-update
  171.3 113.6 %reduce-scatter.8.cloned.1.call-done = f32[128,576]{0,1:T(8,128)} async-done(((f32[128,18432]{0,1:T(8,128)}), f32[128,576]{0,1:T(8,128)}) %reduce-scatter.8.cloned.1.call-update) | async-done | bytes 294928 | tf_op jit(solution)/shard_map/reduce_scatter | solution.py:35
  285.0 154.4 %reduce-scatter.10.cloned.1.call-done = f32[576,128]{1,0:T(8,128)} async-done(((f32[18432,128]{1,0:T(8,128)}), f32[576,128]{1,0:T(8,128)}) %reduce-scatter.10.cloned.1.call-update) | async-done | bytes 294928
  439.4 114.5 %reduce-scatter.6.cloned.1.call-done = f32[16,18432]{1,0:T(8,128)} async-done(((f32[128,18432]{1,0:T(8,128)}), f32[16,18432]{1,0:T(8,128)}) %reduce-scatter.6.cloned.1.call-update) | async-done | bytes 1179664 | tf_op jit(solution)/shard_map/reduce_scatter | solution.py:25
Async XLA Ops:
  7.2 66.2 %all-gather.5.cloned.1.call-start = ((), (), s32[]{:S(2)}) async-start(), calls=%async_computation.4 | async-start | bytes 5308416 | tf_op jit(solution)/shard_map/all_gather | solution.py:9
  7.9 125.6 %all-gather.3.cloned.1.call-start = ((), (), s32[]{:S(2)}) async-start(), calls=%async_computation.3 | async-start | bytes 5308416 | tf_op jit(solution)/shard_map/all_gather | solution.py:10
  8.6 276.3 %reduce-scatter.8.cloned.1.call-start = ((), (), s32[]{:S(2)}) async-start(), calls=%async_computation.6 | async-start | bytes 9732096 | tf_op jit(solution)/shard_map/reduce_scatter | solution.py:35
  141.5 298.0 %reduce-scatter.10.cloned.1.call-start = ((), (), s32[]{:S(2)}) async-start(), calls=%async_computation.7 | async-start | bytes 9732096
  163.8 390.1 %reduce-scatter.6.cloned.1.call-start = ((), (), s32[]{:S(2)}) async-start(), calls=%async_computation.5 | async-start | bytes 10616832 | tf_op jit(solution)/shard_map/reduce_scatter | solution.py:25
Sparse Core Ops, SparseCore 0:
  9.8 63.5 all-gather.4
  75.1 58.3 all-gather.2
  141.6 143.3 reduce-scatter.7
  288.0 151.3 reduce-scatter.9
  442.4 111.4 reduce-scatter.5
where the time goes:
time: 561 us; the launch traced here: 560 us
  waiting for transfers between devices  504 us (90%)
  matrix products  33.2 us (6%)
  between operations  13.8 us (2%)
  local copies, waits for them, and re-layouts  9.65 us (2%)
    unnamed x6, waiting for transfers between devices  156 us
    reduce_scatter x1, waiting for transfers between devices, per_device(): lax.psum_scatter(lax.dot_general(pre_grad, w_in, (((1,), (1,)), ((), ()))...  115 us
    reduce_scatter x1, waiting for transfers between devices, per_device(): lax.psum_scatter(out_grad, ('dcn', 'dp'), scatter_dimension=1, tiled=True)  114 us
    all_gather x1, waiting for transfers between devices, per_device(): lax.all_gather(tokens, 'tp', axis=0, tiled=True)  64.7 us
    all_gather x1, waiting for transfers between devices, per_device(): lax.all_gather(upstream, 'tp', axis=0, tiled=True)  55 us
  transfers between devices with their start and end apart: 5, of which 5 were waited for; matrix products, arithmetic and copies ran while one was open for 6% of the time, Pallas kernels for 0%

commit v1 on v0

v1 whole, which is shorter than its diff:
```python
import functools

import jax
import jax.numpy as jnp
from jax import lax
from jax.experimental import pallas as pl
from jax.experimental.pallas import tpu as pltpu
from jax.sharding import PartitionSpec as P

MESH = pl.DeviceIdType.MESH
F32 = jnp.float32
BF16 = jnp.bfloat16


def mult(value, of):
    return pl.multiple_of(value, of)


def kernel(
    cfg,
    tokens, upstream, w_in, w_out,
    tg_out, ing_out, outg_out,
    tokb, upb, tokT, upT, w1, w2, wo_tmp,
    prep, sibr, urecv, usum, vrecv, pos, gath,
    grad, zsend, zrecv, tgb, tgr, tga, res,
    loc_sem, a2a_send, a2a_recv, ag_send, ag_recv, rs_send, rs_recv,
    sib_send, sib_recv, u_send, u_recv, v_send, v_recv,
):
    NXL, NDP, NZ, NS, T, B, W, HID = cfg
    NP = NXL * NDP
    H = NZ // 2
    R = NP * T
    HR = R // 2
    HB = B // 2
    TS = min(256, HID)
    NT = HID // TS

    z = lax.axis_index("tp")
    dcn = lax.axis_index("dcn")
    dp = lax.axis_index("dp")
    k = dp % 2
    y = (dp // 2) % NS
    x = (dp // (2 * NS)) * NXL + dcn
    me = dcn * NDP + dp
    u = jnp.where(k == 0, x, y)
    v = jnp.where(k == 0, y, x)

    def dev(x_, y_, k_):
        return (x_ % NXL, (x_ // NXL) * (2 * NS) + y_ * 2 + k_, z)

    def dev_i(i_):
        return (i_ // NDP, i_ % NDP, z)

    sib = dev(x, y, 1 - k)

    def u_peer(u_):
        return dev(jnp.where(k == 0, u_, x), jnp.where(k == 0, y, u_), k)

    def v_peer(v_):
        return dev(jnp.where(k == 0, x, v_), jnp.where(k == 0, v_, y), k)

    right = (dcn, dp, (z + 1) % NZ)
    left = (dcn, dp, (z + NZ - 1) % NZ)
    zn = (right, left)

    def lane0(i_):
        return mult(128 * ((B // 64) * (i_ // 2) + (B // 128) * (i_ % 2)), 128)

    row0 = mult(64 * k, 64)
    pad0 = mult(jnp.where(k == 0, B, 0), 64)
    sends = []

    def send(src, dst, ss, rs, to):
        c = pltpu.make_async_remote_copy(
            src_ref=src, dst_ref=dst, send_sem=ss, recv_sem=rs, device_id=to, device_id_type=MESH
        )
        c.start()
        sends.append(c)
        return c

    barrier = pltpu.get_barrier_semaphore()

    @pl.loop(1, NP)
    def _(d):
        pl.semaphore_signal(barrier, inc=1, device_id=dev_i((me + d) % NP), device_id_type=MESH)

    pl.semaphore_signal(barrier, inc=1, device_id=right, device_id_type=MESH)
    if NZ > 2:
        pl.semaphore_signal(barrier, inc=1, device_id=left, device_id_type=MESH)

    my_lane = lane0(me)
    own = pl.ds(mult(128 * z, 128), 128)
    c_win = pltpu.make_async_copy(
        w_in.at[pl.ds(mult(B * me, 64), B), :], w1.at[pl.ds(row0, B), own], loc_sem.at[0]
    )
    c_win.start()
    c_wout = pltpu.make_async_copy(w_out.at[:, pl.ds(my_lane, W)], wo_tmp, loc_sem.at[1])
    c_wout.start()
    my_rows = pl.ds(mult(T * me, T), T)
    c_tok = pltpu.make_async_copy(tokens.at[:, pl.ds(my_lane, W)], tokb.at[my_rows, :], loc_sem.at[2])
    c_tok.start()
    c_up = pltpu.make_async_copy(upstream.at[:, pl.ds(my_lane, W)], upb.at[my_rows, :], loc_sem.at[3])
    c_up.start()
    w1[pl.ds(pad0, 64), :] = jnp.zeros((64, HID), BF16)
    w2[pl.ds(pad0, 64), :] = jnp.zeros((64, HID), BF16)
    c_wout.wait()
    w2[pl.ds(row0, B), own] = jnp.where(
        k == 0, wo_tmp[:, 0:B].T, wo_tmp[:, W - B : W].T
    )
    c_win.wait()
    pl.semaphore_wait(barrier, NP + (1 if NZ > 2 else 0))

    def part(hf):
        return pl.ds(mult(row0 + HB * hf, 16), HB)

    def halves(step, d):
        return (0, 1) if step < H - 1 else (d,)

    def ag_block(w, wi, step, d, hf, start):
        if start:
            blk = (z + NZ - step) % NZ if d == 0 else (z + step) % NZ
        else:
            blk = (z + NZ - 1 - step) % NZ if d == 0 else (z + 1 + step) % NZ
        ref = w.at[part(hf), pl.ds(mult(128 * blk, 128), 128)]
        n = ((wi * 2 + d) * H + step) * 2 + hf
        return ref, ag_send.at[n], ag_recv.at[n]

    def ag_start(w, wi, step):
        for hf in (0, 1):
            for d in (0, 1):
                if hf in halves(step, d):
                    ref, ss, rs = ag_block(w, wi, step, d, hf, True)
                    send(ref, ref, ss, rs, zn[d])

    def ag_wait(w, wi, step, hf, d):
        ref, ss, rs = ag_block(w, wi, step, d, hf, False)
        pltpu.make_async_copy(ref, ref, rs).wait()

    def ag_step(w, wi, step):
        for hf in (0, 1):
            for d in (0, 1):
                if hf in halves(step, d):
                    ag_wait(w, wi, step, hf, d)
                    if step + 1 < H and hf in halves(step + 1, d):
                        ref, ss, rs = ag_block(w, wi, step + 1, d, hf, True)
                        send(ref, ref, ss, rs, zn[d])

    def a2a_start(src, dst, n):
        @pl.loop(1, NP)
        def _(dd):
            to = (me + dd) % NP
            pltpu.make_async_remote_copy(
                src_ref=src.at[:, pl.ds(lane0(to), W)],
                dst_ref=dst.at[my_rows, :],
                send_sem=a2a_send.at[n],
                recv_sem=a2a_recv.at[n],
                device_id=dev_i(to),
                device_id_type=MESH,
            ).start()

    def a2a_wait(buf, n, sems):
        ref = buf.at[pl.ds(0, R - T), :]
        pltpu.make_async_copy(ref, ref, sems.at[n]).wait()

    ag_start(w1, 0, 0)
    a2a_start(tokens, tokb, 0)
    if H > 1:
        ag_step(w1, 0, 0)
    a2a_start(upstream, upb, 1)
    for s in range(1 if H > 1 else 0, H):
        ag_step(w1, 0, s)
        if s == max(H - 2, 0):
            ag_start(w2, 1, 0)
    c_tok.wait()
    a2a_wait(tokb, 0, a2a_recv)

    my_half = mult(HR * k, HR)
    sib_half = mult(HR * (1 - k), HR)
    UR = HR // NS

    def mm_half(lhs, w, n, start):
        @pl.loop(0, NT)
        def _(t):
            cols = pl.ds(mult(TS * t, TS), TS)
            prep[n, pl.ds(start, HR), cols] = jnp.dot(
                lhs[pl.ds(start, HR), :], w[:, cols], preferred_element_type=F32
            )

    def presum_start(lhs, w, n):
        mm_half(lhs, w, n, sib_half)
        rows = prep.at[n, pl.ds(sib_half, HR), :]
        c = send(rows, sibr.at[n], sib_send.at[n], sib_recv.at[n], sib)
        mm_half(lhs, w, n, my_half)
        return c

    def presum_end(c, n):
        c.wait_recv()
        out = []
        for r in list(range(1, NS)) + [0]:
            uu = (u + r) % NS
            rows = pl.ds(mult(my_half + UR * uu, UR), UR)
            loc = pl.ds(mult(UR * uu, UR), UR)
            prep[n, rows, :] += sibr[n, loc, :]
            if r:
                out.append(
                    send(prep.at[n, rows, :], urecv.at[n, r - 1], u_send.at[n, r - 1], u_recv.at[n, r - 1], u_peer(uu))
                )
        return out

    def u_end(cs, n):
        rows = pl.ds(mult(my_half + UR * u, UR), UR)
        for c in cs:
            c.wait_recv()
        tot = prep[n, rows, :]
        for r in range(NS - 1):
            tot = tot + urecv[n, r]
        usum[n] = tot
        out = []
        for r in range(1, NS):
            vv = (v + r) % NS
            out.append(
                send(
                    usum.at[n, pl.ds(mult(T * vv, T), T), :], vrecv.at[n, r - 1],
                    v_send.at[n, r - 1], v_recv.at[n, r - 1], v_peer(vv),
                )
            )
        return out

    def v_end(cs, n):
        for c in cs:
            c.wait_recv()
        tot = usum[n, pl.ds(mult(T * v, T), T), :]
        for r in range(NS - 1):
            tot = tot + vrecv[n, r]
        return tot

    def gv_start(n):
        ref = gath.at[n, pl.ds(mult(my_half + UR * u + T * v, T), T), :]
        return [
            send(ref, ref, v_send.at[2 + n, r - 1], v_recv.at[2 + n, r - 1], v_peer((v + r) % NS))
            for r in range(1, NS)
        ]

    def gu_start(cs, n):
        for c in cs:
            c.wait_recv()
        ref = gath.at[n, pl.ds(mult(my_half + UR * u, UR), UR), :]
        return [
            send(ref, ref, u_send.at[2 + n, r - 1], u_recv.at[2 + n, r - 1], u_peer((u + r) % NS))
            for r in range(1, NS)
        ]

    def gs_start(cs, n):
        for c in cs:
            c.wait_recv()
        ref = gath.at[n, pl.ds(my_half, HR), :]
        return send(ref, ref, sib_send.at[2 + n], sib_recv.at[2 + n], sib)

    MT = W // 2

    def grad_mm(lhsT, n):
        @pl.loop(0, NT)
        def _(t):
            cols = pl.ds(mult(TS * t, TS), TS)
            for m in range(2):
                grad[n, pl.ds(MT * m, MT), cols] = jnp.dot(
                    lhsT[pl.ds(MT * m, MT), :], gath[n, :, cols], preferred_element_type=F32
                )

    def grad_block(n, blk, hf):
        return grad[n, part(hf), pl.ds(mult(128 * blk, 128), 128)]

    def rs_idx(n, d, step):
        return (n * 2 + d) * H + step

    def rs_halves(step, d):
        return (d,) if step == 0 else (0, 1)

    def rs_send_block(n, d, step, hf, val):
        q = rs_idx(n, d, step)
        rows = pl.ds(HB * hf, HB)
        zsend[q, rows, :] = val.astype(BF16)
        send(
            zsend.at[q, rows, :], zrecv.at[q, rows, :],
            rs_send.at[q * 2 + hf], rs_recv.at[q * 2 + hf], zn[d],
        )

    def rs_get(n, d, step, hf):
        q = rs_idx(n, d, step)
        rows = pl.ds(HB * hf, HB)
        ref = zrecv.at[q, rows, :]
        pltpu.make_async_copy(ref, ref, rs_recv.at[q * 2 + hf]).wait()
        return zrecv[q, rows, :].astype(F32)

    def rs_dest(d, step):
        return (z + H - step) % NZ if d == 0 else (z + NZ - H + step) % NZ

    def rs_step(n, step):
        order = ((0, 0), (1, 1), (0, 1), (1, 0))
        for d, hf in order:
            if hf in rs_halves(step, d):
                val = grad_block(n, rs_dest(d, step), hf)
                if step >= 1 and hf in rs_halves(step - 1, d):
                    val = val + rs_get(n, d, step - 1, hf)
                rs_send_block(n, d, step, hf, val)

    def rs_end(n):
        for hf in (0, 1):
            val = grad_block(n, z, hf)
            for d in (0, 1):
                if hf in rs_halves(H - 1, d):
                    val = val + rs_get(n, d, H - 1, hf)
            res[n, pl.ds(HB * hf, HB), :] = val

    c = presum_start(tokb, w1, 0)
    if H > 1:
        ag_step(w2, 1, 0)
    cu = presum_end(c, 0)
    for s in range(1, H - 1):
        ag_step(w2, 1, s)
    tokT[...] = tokb[...].T
    cv = u_end(cu, 0)
    ag_step(w2, 1, H - 1)
    c_up.wait()
    a2a_wait(upb, 1, a2a_recv)
    positive = jnp.maximum(v_end(cv, 0), 0.0)
    pos[...] = positive
    gath[0, pl.ds(mult(my_half + UR * u + T * v, T), T), :] = (positive * positive).astype(BF16)
    gv = gv_start(0)
    c = presum_start(upb, w2, 1)
    gu = gu_start(gv, 0)
    cu = presum_end(c, 1)
    gs = gs_start(gu, 0)
    upT[...] = upb[...].T
    gs.wait_recv()
    grad_mm(upT, 0)
    rs_step(0, 0)
    cv = u_end(cu, 1)
    pg = v_end(cv, 1) * 2.0 * pos[...]
    gath[1, pl.ds(mult(my_half + UR * u + T * v, T), T), :] = pg.astype(BF16)
    gv = gv_start(1)
    if H > 1:
        rs_step(0, 1)
    gu = gu_start(gv, 1)
    if H > 2:
        rs_step(0, 2)
    gs = gs_start(gu, 1)
    for s in range(3, H):
        rs_step(0, s)
    gs.wait_recv()
    grad_mm(tokT, 1)
    rs_step(1, 0)

    TR = min(128, R)

    @pl.loop(0, R // TR)
    def _(t):
        rows = pl.ds(mult(TR * t, TR), TR)
        tgb[rows, :] = lax.dot_general(
            gath[1, rows, :], w1[...], (((1,), (1,)), ((), ())), preferred_element_type=F32
        ).astype(BF16)

    @pl.loop(1, NP)
    def _(dd):
        to = (me + dd) % NP
        pltpu.make_async_remote_copy(
            src_ref=tgb.at[pl.ds(mult(T * to, T), T), :],
            dst_ref=tgr.at[my_rows, :],
            send_sem=a2a_send.at[2],
            recv_sem=a2a_recv.at[2],
            device_id=dev_i(to),
            device_id_type=MESH,
        ).start()

    tgr[my_rows, :] = tgb[my_rows, :]
    if H > 1:
        rs_step(1, 1)
    rs_end(0)
    c_o = pltpu.make_async_copy(res.at[0], outg_out, loc_sem.at[0])
    c_o.start()
    if H > 2:
        rs_step(1, 2)
    a2a_wait(tgr, 2, a2a_recv)
    FT = (B // 128) * 128

    @pl.loop(0, NP // 2)
    def _(p):
        base = 2 * B * p
        r0 = pl.ds(mult(2 * T * p, 2 * T), T)
        r1 = pl.ds(mult(2 * T * p + T, T), T)
        tga[:, pl.ds(mult(base, 128), FT)] = tgr[r0, 0:FT]
        tga[:, pl.ds(mult(base + FT, 128), 128)] = tgr[r0, FT:W] + tgr[r1, 0:128]
        tga[:, pl.ds(mult(base + FT + 128, 128), FT)] = tgr[r1, 128:W]

    c_t = pltpu.make_async_copy(tga, tg_out, loc_sem.at[1])
    c_t.start()
    for s in range(3, H):
        rs_step(1, s)
    rs_end(1)
    c_i = pltpu.make_async_copy(res.at[1], ing_out, loc_sem.at[2])
    c_i.start()

    for c in sends:
        c.wait_send()
    a2a_wait(tokb, 0, a2a_send)
    a2a_wait(upb, 1, a2a_send)
    a2a_wait(tgb, 2, a2a_send)
    c_o.wait()
    c_t.wait()
    c_i.wait()


def make(mesh):
    NXL, NDP, NZ = mesh.shape["dcn"], mesh.shape["dp"], mesh.shape["tp"]
    NP = NXL * NDP
    NS = 1
    while NS * NS * 2 < NP:
        NS += 1

    def per_device(tokens, upstream, w_in, w_out):
        T, D = tokens.shape
        B = D // NP
        W = B + 64
        HID = 128 * NZ
        H = NZ // 2
        R = NP * T
        HR = R // 2
        UR = HR // NS
        cfg = (NXL, NDP, NZ, NS, T, B, W, HID)
        DMA = pltpu.SemaphoreType.DMA
        scratch = [
            pltpu.VMEM((R, W), BF16),
            pltpu.VMEM((R, W), BF16),
            pltpu.VMEM((W, R), BF16),
            pltpu.VMEM((W, R), BF16),
            pltpu.VMEM((W, HID), BF16),
            pltpu.VMEM((W, HID), BF16),
            pltpu.VMEM((128, W), BF16),
            pltpu.VMEM((2, R, HID), F32),
            pltpu.VMEM((2, HR, HID), F32),
            pltpu.VMEM((2, NS - 1, UR, HID), F32),
            pltpu.VMEM((2, UR, HID), F32),
            pltpu.VMEM((2, NS - 1, T, HID), F32),
            pltpu.VMEM((T, HID), F32),
            pltpu.VMEM((2, R, HID), BF16),
            pltpu.VMEM((2, W, HID), F32),
            pltpu.VMEM((4 * H, B, 128), BF16),
            pltpu.VMEM((4 * H, B, 128), BF16),
            pltpu.VMEM((R, W), BF16),
            pltpu.VMEM((R, W), BF16),
            pltpu.VMEM((T, D), BF16),
            pltpu.VMEM((2, B, 128), F32),
            DMA((4,)),
            DMA((3,)),
            DMA((3,)),
            DMA((8 * H,)),
            DMA((8 * H,)),
            DMA((8 * H,)),
            DMA((8 * H,)),
            DMA((4,)),
            DMA((4,)),
            DMA((4, NS - 1)),
            DMA((4, NS - 1)),
            DMA((4, NS - 1)),
            DMA((4, NS - 1)),
        ]
        tg, ing, outg = pl.pallas_call(
            functools.partial(kernel, cfg),
            out_shape=(
                jax.ShapeDtypeStruct((T, D), BF16),
                jax.ShapeDtypeStruct((B, 128), F32),
                jax.ShapeDtypeStruct((B, 128), F32),
            ),
            in_specs=[pl.BlockSpec(memory_space=pl.ANY)] * 4,
            out_specs=tuple([pl.BlockSpec(memory_space=pl.ANY)] * 3),
            scratch_shapes=scratch,
            compiler_params=pltpu.CompilerParams(
                collective_id=0, has_side_effects=True, vmem_limit_bytes=56 * 2**20
            ),
        )(tokens, upstream, w_in, w_out)
        return tg.astype(F32), ing, outg.T

    return per_device


def solution(mesh):
    placed = (
        P(("dcn", "dp", "tp"), None),
        P(("dcn", "dp", "tp"), None),
        P(None, "tp"),
        P("tp", None),
    )
    return jax.shard_map(
        make(mesh),
        mesh=mesh,
        in_specs=placed,
        out_specs=(P(("dcn", "dp", "tp"), None), P(("dcn", "dp"), "tp"), P("tp", ("dcn", "dp"))),
        check_vma=False,
    )
```

time: 561 us -> 107 us (0.19)
  waiting for transfers between devices: 504 us -> 0 us
  Pallas kernels: 0 us -> 100 us
  matrix products: 33.2 us -> 0 us
  between operations: 13.8 us -> 0.64 us
  local copies, waits for them, and re-layouts: 9.65 us -> 3.39 us
    reduce_scatter x2 -> x0, waiting for transfers between devices: 228 us -> none  [the longest x1 115 us: per_device(): lax.psum_scatter(lax.dot_general(pre_grad, w_in, (((1,), (1,)), ((), ()))...]
    unnamed x6 -> x0, waiting for transfers between devices: 156 us -> none
    all_gather x2 -> x0, waiting for transfers between devices: 120 us -> none  [the longest x1 64.7 us: per_device(): lax.all_gather(tokens, 'tp', axis=0, tiled=True)]
    pallas_call x0 -> x1, Pallas kernels: none -> 100 us  [per_device(): pl.pallas_call(functools.partial(kernel, cfg), out_shape=(jax.ShapeDtypeS...]
    dot_general x5 -> x0, matrix products: 33.2 us -> none  [the longest x1 7.92 us: per_device(): lax.dot_general(act, seq_grad, (((0,), (0,)), ((), ())), preferred_elemen...]
    unnamed x1 -> x2, local copies, waits for them, and re-layouts: 9.65 us -> 3.39 us
  transfers between devices with their start and end apart: 5 -> 0, of which waited for: 5 -> 0; matrix products, arithmetic and copies ran while one was open for 6% -> 0% of each run, Pallas kernels for 0% -> 0%
where the time goes in v1:
time: 107 us; the launch traced here: 106 us
  Pallas kernels  100 us (93%)
  local copies, waits for them, and re-layouts  3.39 us (3%)
  other arithmetic  2.15 us (2%)
    pallas_call x1, Pallas kernels, per_device(): pl.pallas_call(functools.partial(kernel, cfg), out_shape=(jax.ShapeDtypeS...  100 us
    unnamed x2, local copies, waits for them, and re-layouts  3.39 us
    convert_element_type x1, other arithmetic, per_device(): return (tg.astype(F32), ing, outg.T)  2.15 us

profile of v1, /device:TPU:1, one launch (start us, length us, event | category | flops | bytes accessed | tf_op | source)
XLA Modules:
  0.0 106.3 jit_solution(17606269101540379783)
XLA Ops:
  0.6 100.2 %shard_map.67 = (bf16[16,18432]{1,0:T(8,128)(2,1)}, f32[576,128]{1,0:T(8,128)}, f32[576,128]{1,0:T(8,128)}) custom-call(bf16[16,18432]{1,0:T(8,128)(2,1)} %tokens.1, bf16[16,18432]{1,0:T(8,128)(2,1)} %upstream.1, bf16[18432,128]{1,0:T(8,128)(2,1)} %w_in.1, bf16[128,18432]{1,0:T(8,128)(2,1)} %w_out.1), custom_call_target="tpu_custom_call" | custom-call | tf_op jit(solution)/shard_map/pallas_call | solution.py:467
  100.8 2.2 %convert_element_type.3 = f32[16,18432]{1,0:T(8,128)} convert(bf16[16,18432]{1,0:T(8,128)(2,1)} %get-tuple-element.6) | non-fusion elementwise | flops 294912 | bytes 1769472 | tf_op jit(solution)/shard_map/convert_element_type | solution.py:481
  102.9 1.7 %copy.9 = f32[576,128]{1,0:T(8,128)} copy(f32[576,128]{1,0:T(8,128)} %get-tuple-element.13) | data formatting | bytes 589824
  104.6 1.7 %copy.10 = f32[128,576]{0,1:T(8,128)} copy(f32[128,576]{0,1:T(8,128)} %bitcast.1) | data formatting | bytes 589824

commit v2 on v0

v2 whole, which is shorter than its diff:
```python
import functools

import jax
import jax.numpy as jnp
from jax import lax
from jax.experimental import pallas as pl
from jax.experimental.pallas import tpu as pltpu
from jax.sharding import PartitionSpec as P

MESH = pl.DeviceIdType.MESH
F32 = jnp.float32
BF16 = jnp.bfloat16


def mult(value, of):
    return pl.multiple_of(value, of)


def kernel(
    cfg,
    tokens, upstream, w_in, w_out,
    tg_out, ing_out, outg_out,
    tokb, upb, tokT, upT, w1, w2, w1T, wo_tmp,
    prep, sibr, urecv, usum, vrecv, pos, gath,
    grad, zsend, zrecv, tgb, tgr, tga, res,
    loc_sem, a2a_send, a2a_recv, ag_send, ag_recv, rs_send, rs_recv,
    sib_send, sib_recv, u_send, u_recv, v_send, v_recv,
):
    NXL, NDP, NZ, NS, T, B, W, HID = cfg
    NP = NXL * NDP
    H = NZ // 2
    R = NP * T
    HR = R // 2
    HB = B // 2
    TS = min(256, HID)
    NT = HID // TS

    z = lax.axis_index("tp")
    dcn = lax.axis_index("dcn")
    dp = lax.axis_index("dp")
    k = dp % 2
    y = (dp // 2) % NS
    x = (dp // (2 * NS)) * NXL + dcn
    me = dcn * NDP + dp
    u = jnp.where(k == 0, x, y)
    v = jnp.where(k == 0, y, x)

    def dev(x_, y_, k_):
        return (x_ % NXL, (x_ // NXL) * (2 * NS) + y_ * 2 + k_, z)

    def dev_i(i_):
        return (i_ // NDP, i_ % NDP, z)

    sib = dev(x, y, 1 - k)

    def u_peer(u_):
        return dev(jnp.where(k == 0, u_, x), jnp.where(k == 0, y, u_), k)

    def v_peer(v_):
        return dev(jnp.where(k == 0, x, v_), jnp.where(k == 0, v_, y), k)

    right = (dcn, dp, (z + 1) % NZ)
    left = (dcn, dp, (z + NZ - 1) % NZ)
    zn = (right, left)

    def lane0(i_):
        return mult(128 * ((B // 64) * (i_ // 2) + (B // 128) * (i_ % 2)), 128)

    row0 = mult(64 * k, 64)
    pad0 = mult(jnp.where(k == 0, B, 0), 64)
    sends = []

    def send(src, dst, ss, rs, to):
        c = pltpu.make_async_remote_copy(
            src_ref=src, dst_ref=dst, send_sem=ss, recv_sem=rs, device_id=to, device_id_type=MESH
        )
        c.start()
        sends.append(c)
        return c

    def landed(ref, sem):
        pltpu.make_async_copy(ref, ref, sem).wait()

    def drain():
        while sends:
            sends.pop(0).wait_send()

    def slot(m):
        if abs(m) == H:
            return NZ - 1
        return 2 * m if m >= 0 else -2 * m - 1

    def lanes(s):
        return pl.ds(128 * s, 128)

    barrier = pltpu.get_barrier_semaphore()
    my_lane = lane0(me)
    my_rows = pl.ds(mult(T * me, T), T)

    def entry():
        pl.semaphore_signal(barrier, inc=1, device_id=right, device_id_type=MESH)
        if NZ > 2:
            pl.semaphore_signal(barrier, inc=1, device_id=left, device_id_type=MESH)

        @pl.loop(1, NP)
        def _(d):
            pl.semaphore_signal(barrier, inc=1, device_id=dev_i((me + d) % NP), device_id_type=MESH)

    c_win = pltpu.make_async_copy(
        w_in.at[pl.ds(mult(B * me, 64), B), :], w1.at[pl.ds(row0, B), lanes(0)], loc_sem.at[0]
    )
    c_wout = pltpu.make_async_copy(w_out.at[:, pl.ds(my_lane, W)], wo_tmp, loc_sem.at[1])
    c_tok = pltpu.make_async_copy(tokens.at[:, pl.ds(my_lane, W)], tokb.at[my_rows, :], loc_sem.at[2])
    c_up = pltpu.make_async_copy(upstream.at[:, pl.ds(my_lane, W)], upb.at[my_rows, :], loc_sem.at[3])

    def entry_wait():
        c_win.wait()
        pl.semaphore_wait(barrier, NP + (1 if NZ > 2 else 0))

    def own_wout():
        w1[pl.ds(pad0, 64), :] = jnp.zeros((64, HID), BF16)
        w2[pl.ds(pad0, 64), :] = jnp.zeros((64, HID), BF16)
        c_wout.wait()
        w2[pl.ds(row0, B), lanes(0)] = jnp.where(k == 0, wo_tmp[:, 0:B].T, wo_tmp[:, W - B : W].T)

    def part(hf):
        return pl.ds(mult(row0 + HB * hf, 16), HB)

    def halves(step, d):
        return (0, 1) if step < H - 1 else (d,)

    def ag_send_one(wi, step, d, hf):
        w = (w1, w2)[wi]
        sg = 1 if d else -1
        n = ((wi * 2 + d) * H + step) * 2 + hf
        send(
            w.at[part(hf), lanes(slot(sg * step))], w.at[part(hf), lanes(slot(sg * (step + 1)))],
            ag_send.at[n], ag_recv.at[n], zn[d],
        )

    def ag_start(wi):
        for hf in (0, 1):
            for d in (0, 1):
                if hf in halves(0, d):
                    ag_send_one(wi, 0, d, hf)

    def ag(wi, step, hf):
        if step >= H:
            return
        w = (w1, w2)[wi]
        for d in (0, 1):
            if hf in halves(step, d):
                n = ((wi * 2 + d) * H + step) * 2 + hf
                landed(w.at[part(hf), lanes(slot((1 if d else -1) * (step + 1)))], ag_recv.at[n])
                if step + 1 < H and hf in halves(step + 1, d):
                    ag_send_one(wi, step + 1, d, hf)

    def a2a_start(src, dst, n, lo, hi):
        @pl.loop(lo, hi)
        def _(dd):
            to = (me + dd) % NP
            pltpu.make_async_remote_copy(
                src_ref=src.at[:, pl.ds(lane0(to), W)],
                dst_ref=dst.at[my_rows, :],
                send_sem=a2a_send.at[n],
                recv_sem=a2a_recv.at[n],
                device_id=dev_i(to),
                device_id_type=MESH,
            ).start()

    def a2a_wait(buf, n, sems):
        landed(buf.at[pl.ds(0, R - T), :], sems.at[n])

    my_half = mult(HR * k, HR)
    sib_half = mult(HR * (1 - k), HR)
    UR = HR // NS
    mine = pl.ds(mult(my_half + UR * u + T * v, T), T)
    pend = {}

    def chunk(c):
        return pl.ds(TS * c, TS)

    def mm_part(n, c, start):
        lhs, w = ((tokb, w1), (upb, w2))[n]
        prep[n, pl.ds(start, HR), chunk(c)] = jnp.dot(
            lhs[pl.ds(start, HR), :], w[:, chunk(c)], preferred_element_type=F32
        )

    def P_(n, c):
        if c >= NT:
            return
        q = n * NT + c
        mm_part(n, c, sib_half)
        pend["s", n, c] = send(
            prep.at[n, pl.ds(sib_half, HR), chunk(c)], sibr.at[n, :, chunk(c)], sib_send.at[q], sib_recv.at[q], sib
        )
        mm_part(n, c, my_half)

    def S_(n, c):
        if c >= NT:
            return
        q = n * NT + c
        pend["s", n, c].wait_recv()
        out = []
        for r in [2, 1, 3, 0] if NS == 4 else list(range(1, NS)) + [0]:
            uu = (u + r) % NS
            rows = pl.ds(mult(my_half + UR * uu, UR), UR)
            prep[n, rows, chunk(c)] += sibr[n, pl.ds(mult(UR * uu, UR), UR), chunk(c)]
            if r:
                out.append(
                    send(
                        prep.at[n, rows, chunk(c)], urecv.at[n, r - 1, :, chunk(c)],
                        u_send.at[q, r - 1], u_recv.at[q, r - 1], u_peer(uu),
                    )
                )
        pend["u", n, c] = out

    def U_(n, c):
        if c >= NT:
            return
        q = n * NT + c
        for d in pend["u", n, c]:
            d.wait_recv()
        tot = prep[n, pl.ds(mult(my_half + UR * u, UR), UR), chunk(c)]
        for r in range(NS - 1):
            tot = tot + urecv[n, r, :, chunk(c)]
        usum[n, :, chunk(c)] = tot
        pend["v", n, c] = [
            send(
                usum.at[n, pl.ds(mult(T * ((v + r) % NS), T), T), chunk(c)], vrecv.at[n, r - 1, :, chunk(c)],
                v_send.at[q, r - 1], v_recv.at[q, r - 1], v_peer((v + r) % NS),
            )
            for r in range(1, NS)
        ]

    def V_(n, c):
        if c >= NT:
            return
        for d in pend["v", n, c]:
            d.wait_recv()
        tot = usum[n, pl.ds(mult(T * v, T), T), chunk(c)]
        for r in range(NS - 1):
            tot = tot + vrecv[n, r, :, chunk(c)]
        if n == 0:
            positive = jnp.maximum(tot, 0.0)
            pos[:, chunk(c)] = positive
            gath[0, mine, chunk(c)] = (positive * positive).astype(BF16)
        else:
            gath[1, mine, chunk(c)] = (tot * 2.0 * pos[:, chunk(c)]).astype(BF16)
        if (c + 1) % CG == 0:
            GV0(n, c // CG)

    CG = 2 if NT % 2 == 0 else 1
    NG = NT // CG

    def group(g):
        return pl.ds(TS * CG * g, TS * CG)

    def gq(n, g):
        return 2 * NT + n * NG + g

    def GV0(n, g):
        ref = gath.at[n, mine, group(g)]
        pend["gv", n, g] = [
            send(ref, ref, v_send.at[gq(n, g), r - 1], v_recv.at[gq(n, g), r - 1], v_peer((v + r) % NS))
            for r in range(1, NS)
        ]

    def GV(n, g):
        if g >= NG:
            return
        for d in pend["gv", n, g]:
            d.wait_recv()
        ref = gath.at[n, pl.ds(mult(my_half + UR * u, UR), UR), group(g)]
        pend["gu", n, g] = [
            send(ref, ref, u_send.at[gq(n, g), r - 1], u_recv.at[gq(n, g), r - 1], u_peer((u + r) % NS))
            for r in range(1, NS)
        ]

    def GU(n, g):
        if g >= NG:
            return
        for d in pend["gu", n, g]:
            d.wait_recv()
        ref = gath.at[n, pl.ds(my_half, HR), group(g)]
        pend["gs", n, g] = send(ref, ref, sib_send.at[gq(n, g)], sib_recv.at[gq(n, g)], sib)

    def GS(n, g):
        if g >= NG:
            return
        pend["gs", n, g].wait_recv()

    MT = W // 2

    def grad_mm(n, c):
        if c >= NT:
            return
        lhsT = (upT, tokT)[n]

        @pl.loop(0, 2)
        def _(m):
            rows = pl.ds(mult(MT * m, MT), MT)
            grad[n, rows, chunk(c)] = jnp.dot(
                lhsT[rows, :], gath[n, :, chunk(c)], preferred_element_type=F32
            )

    def rs_dest(d, step):
        m = H - step
        return slot(m) if d == 0 else slot(-m)

    def rs_halves(step, d):
        return (d,) if step == 0 else (0, 1)

    def rs_get(n, d, step, hf):
        q = (n * 2 + d) * H + step
        rows = pl.ds(HB * hf, HB)
        landed(zrecv.at[q, rows, :], rs_recv.at[q * 2 + hf])
        return zrecv[q, rows, :].astype(F32)

    def rs_one(n, step, d, hf):
        q = (n * 2 + d) * H + step
        val = grad[n, part(hf), lanes(rs_dest(d, step))]
        if step >= 1 and hf in rs_halves(step - 1, d):
            val = val + rs_get(n, d, step - 1, hf)
        rows = pl.ds(HB * hf, HB)
        zsend[q, rows, :] = val.astype(BF16)
        send(
            zsend.at[q, rows, :], zrecv.at[q, rows, :],
            rs_send.at[q * 2 + hf], rs_recv.at[q * 2 + hf], zn[d],
        )

    def RS(n, step):
        if step >= H:
            return
        if step == 0:
            rs_one(n, 0, 0, 0)
            rs_one(n, 0, 1, 1)
            if H > 1:
                rs_one(n, 1, 0, 1)
                rs_one(n, 1, 1, 0)
        elif step == 1:
            rs_one(n, 1, 0, 0)
            rs_one(n, 1, 1, 1)
        else:
            rs_one(n, step, 0, 1)
            rs_one(n, step, 1, 0)
            rs_one(n, step, 0, 0)
            rs_one(n, step, 1, 1)

    def RS_end(n):
        for hf in (0, 1):
            val = grad[n, part(hf), lanes(0)]
            for d in (0, 1):
                if hf in rs_halves(H - 1, d):
                    val = val + rs_get(n, d, H - 1, hf)
            res[n, pl.ds(HB * hf, HB), :] = val

    def tg_mm(lo, hi):
        @pl.loop(lo * R // 4 // TR, hi * R // 4 // TR)
        def _(t):
            rows = pl.ds(mult(TR * t, TR), TR)
            tgb[rows, :] = jnp.dot(gath[1, rows, :], w1T[...], preferred_element_type=F32).astype(BF16)

    TR = min(128, R // 4)

    def tg_start():
        @pl.loop(1, NP)
        def _(dd):
            to = (me + dd) % NP
            pltpu.make_async_remote_copy(
                src_ref=tgb.at[pl.ds(mult(T * to, T), T), :],
                dst_ref=tgr.at[my_rows, :],
                send_sem=a2a_send.at[2],
                recv_sem=a2a_recv.at[2],
                device_id=dev_i(to),
                device_id_type=MESH,
            ).start()

        tgr[my_rows, :] = tgb[my_rows, :]

    FT = (B // 128) * 128

    def tg_end():
        a2a_wait(tgr, 2, a2a_recv)

        @pl.loop(0, NP // 2)
        def _(p):
            base = 2 * B * p
            r0 = pl.ds(mult(2 * T * p, 2 * T), T)
            r1 = pl.ds(mult(2 * T * p + T, T), T)
            tga[:, pl.ds(mult(base, 128), FT)] = tgr[r0, 0:FT]
            tga[:, pl.ds(mult(base + FT, 128), 128)] = tgr[r0, FT:W] + tgr[r1, 0:128]
            tga[:, pl.ds(mult(base + FT + 128, 128), FT)] = tgr[r1, 128:W]

    def transpose(dst, src):
        dst[...] = src[...].T

    entry()
    for c in (c_win, c_wout, c_tok, c_up):
        c.start()
    entry_wait()
    ag_start(0)
    a2a_start(tokens, tokb, 0, 1, NP)
    own_wout()
    ag(0, 0, 0)
    ag(0, 0, 1)
    a2a_start(upstream, upb, 1, 1, NP // 2)
    ag(0, 1, 0)
    ag(0, 1, 1)
    c_tok.wait()
    a2a_wait(tokb, 0, a2a_recv)
    P_(0, 0)
    ag(0, 2, 0)
    P_(0, 1)
    S_(0, 0)
    ag(0, 2, 1)
    ag_start(1)
    P_(0, 2)
    S_(0, 1)
    ag(0, 3, 0)
    ag(0, 3, 1)
    P_(0, 3)
    S_(0, 2)
    U_(0, 0)
    S_(0, 3)
    a2a_start(upstream, upb, 1, NP // 2, NP)
    ag(1, 0, 0)
    U_(0, 1)
    V_(0, 0)
    ag(1, 0, 1)
    U_(0, 2)
    V_(0, 1)
    U_(0, 3)
    ag(1, 1, 0)
    V_(0, 2)
    V_(0, 3)
    ag(1, 1, 1)
    GV(0, 0)
    transpose(tokT, tokb)
    GV(0, 1)
    ag(1, 2, 0)
    GU(0, 0)
    transpose(w1T, w1)
    ag(1, 2, 1)
    GU(0, 1)
    c_up.wait()
    a2a_wait(upb, 1, a2a_recv)
    P_(1, 0)
    P_(1, 1)
    transpose(upT, upb)
    GS(0, 0)
    grad_mm(0, 0)
    grad_mm(0, 1)
    S_(1, 0)
    P_(1, 2)
    GS(0, 1)
    grad_mm(0, 3)
    grad_mm(0, 2)
    RS(0, 0)
    S_(1, 1)
    ag(1, 3, 0)
    ag(1, 3, 1)
    P_(1, 3)
    S_(1, 2)
    U_(1, 0)
    S_(1, 3)
    U_(1, 1)
    V_(1, 0)
    RS(0, 1)
    U_(1, 2)
    V_(1, 1)
    U_(1, 3)
    V_(1, 2)
    V_(1, 3)
    GV(1, 0)
    RS(0, 2)
    GV(1, 1)
    GU(1, 0)
    RS(0, 3)
    GU(1, 1)
    GS(1, 0)
    GS(1, 1)
    for c in range(NT - 1, max(NT - 3, -1), -1):
        grad_mm(1, c)
    RS(1, 0)
    for c in range(NT - 2):
        grad_mm(1, c)
    tg_mm(0, 2)
    RS(1, 1)
    tg_mm(2, 4)
    tg_start()
    RS_end(0)
    c_o = pltpu.make_async_copy(res.at[0], outg_out, loc_sem.at[0])
    c_o.start()
    RS(1, 2)
    drain()
    a2a_wait(tokb, 0, a2a_send)
    a2a_wait(upb, 1, a2a_send)
    RS(1, 3)
    tg_end()
    c_t = pltpu.make_async_copy(tga, tg_out, loc_sem.at[1])
    c_t.start()
    RS_end(1)
    c_i = pltpu.make_async_copy(res.at[1], ing_out, loc_sem.at[2])
    c_i.start()
    drain()
    a2a_wait(tgb, 2, a2a_send)
    c_o.wait()
    c_t.wait()
    c_i.wait()


def finish(tg, ing, outg, tg_o, ing_o, outg_o, tb, tf, ob, ot, sem):
    NC = 4
    D = tb.shape[1]
    C = D // NC
    c_o = pltpu.make_async_copy(outg, ob, sem.at[0])
    c_o.start()
    c_i = pltpu.make_async_copy(ing, ing_o, sem.at[1])
    c_i.start()
    ins = [pltpu.make_async_copy(tg.at[:, pl.ds(C * c, C)], tb.at[:, pl.ds(C * c, C)], sem.at[2 + c]) for c in range(NC)]
    for c in ins:
        c.start()
    outs = []
    for n in range(NC):
        ins[n].wait()
        cols = pl.ds(C * n, C)
        tf[:, cols] = tb[:, cols].astype(F32)
        o = pltpu.make_async_copy(tf.at[:, cols], tg_o.at[:, cols], sem.at[2 + NC + n])
        o.start()
        outs.append(o)
    c_o.wait()
    ot[...] = ob[...].T
    o = pltpu.make_async_copy(ot, outg_o, sem.at[2 + 2 * NC])
    o.start()
    outs.append(o)
    c_i.wait()
    for o in outs:
        o.wait()


def make(mesh):
    NXL, NDP, NZ = mesh.shape["dcn"], mesh.shape["dp"], mesh.shape["tp"]
    NP = NXL * NDP
    NS = 1
    while NS * NS * 2 < NP:
        NS += 1

    def per_device(tokens, upstream, w_in, w_out):
        T, D = tokens.shape
        B = D // NP
        W = B + 64
        HID = 128 * NZ
        H = NZ // 2
        R = NP * T
        HR = R // 2
        UR = HR // NS
        cfg = (NXL, NDP, NZ, NS, T, B, W, HID)
        NQ = 4 * (HID // min(256, HID))
        DMA = pltpu.SemaphoreType.DMA
        scratch = [
            pltpu.VMEM((R, W), BF16),
            pltpu.VMEM((R, W), BF16),
            pltpu.VMEM((W, R), BF16),
            pltpu.VMEM((W, R), BF16),
            pltpu.VMEM((W, HID), BF16),
            pltpu.VMEM((W, HID), BF16),
            pltpu.VMEM((HID, W), BF16),
            pltpu.VMEM((128, W), BF16),
            pltpu.VMEM((2, R, HID), F32),
            pltpu.VMEM((2, HR, HID), F32),
            pltpu.VMEM((2, NS - 1, UR, HID), F32),
            pltpu.VMEM((2, UR, HID), F32),
            pltpu.VMEM((2, NS - 1, T, HID), F32),
            pltpu.VMEM((T, HID), F32),
            pltpu.VMEM((2, R, HID), BF16),
            pltpu.VMEM((2, W, HID), F32),
            pltpu.VMEM((4 * H, B, 128), BF16),
            pltpu.VMEM((4 * H, B, 128), BF16),
            pltpu.VMEM((R, W), BF16),
            pltpu.VMEM((R, W), BF16),
            pltpu.VMEM((T, D), BF16),
            pltpu.VMEM((2, B, 128), F32),
            DMA((4,)),
            DMA((3,)),
            DMA((3,)),
            DMA((8 * H,)),
            DMA((8 * H,)),
            DMA((8 * H,)),
            DMA((8 * H,)),
            DMA((NQ,)),
            DMA((NQ,)),
            DMA((NQ, NS - 1)),
            DMA((NQ, NS - 1)),
            DMA((NQ, NS - 1)),
            DMA((NQ, NS - 1)),
        ]
        tg, ing, outg = pl.pallas_call(
            functools.partial(kernel, cfg),
            out_shape=(
                jax.ShapeDtypeStruct((T, D), BF16),
                jax.ShapeDtypeStruct((B, 128), F32),
                jax.ShapeDtypeStruct((B, 128), F32),
            ),
            in_specs=[pl.BlockSpec(memory_space=pl.ANY)] * 4,
            out_specs=tuple([pl.BlockSpec(memory_space=pl.ANY)] * 3),
            scratch_shapes=scratch,
            compiler_params=pltpu.CompilerParams(
                collective_id=0, has_side_effects=True, vmem_limit_bytes=56 * 2**20
            ),
        )(tokens, upstream, w_in, w_out)
        return pl.pallas_call(
            finish,
            out_shape=(
                jax.ShapeDtypeStruct((T, D), F32),
                jax.ShapeDtypeStruct((B, 128), F32),
                jax.ShapeDtypeStruct((128, B), F32),
            ),
            in_specs=[pl.BlockSpec(memory_space=pl.ANY)] * 3,
            out_specs=tuple([pl.BlockSpec(memory_space=pl.ANY)] * 3),
            scratch_shapes=[
                pltpu.VMEM((T, D), BF16),
                pltpu.VMEM((T, D), F32),
                pltpu.VMEM((B, 128), F32),
                pltpu.VMEM((128, B), F32),
                DMA((11,)),
            ],
            compiler_params=pltpu.CompilerParams(vmem_limit_bytes=16 * 2**20),
        )(tg, ing, outg)

    return per_device


def solution(mesh):
    placed = (
        P(("dcn", "dp", "tp"), None),
        P(("dcn", "dp", "tp"), None),
        P(None, "tp"),
        P("tp", None),
    )
    return jax.shard_map(
        make(mesh),
        mesh=mesh,
        in_specs=placed,
        out_specs=(P(("dcn", "dp", "tp"), None), P(("dcn", "dp"), "tp"), P("tp", ("dcn", "dp"))),
        check_vma=False,
    )
```

time: 561 us -> 103 us (0.18)
  waiting for transfers between devices: 504 us -> 0 us
  Pallas kernels: 0 us -> 98 us
  matrix products: 33.2 us -> 0 us
  between operations: 13.8 us -> 0.66 us
  local copies, waits for them, and re-layouts: 9.65 us -> 3.84 us
    reduce_scatter x2 -> x0, waiting for transfers between devices: 228 us -> none  [the longest x1 115 us: per_device(): lax.psum_scatter(lax.dot_general(pre_grad, w_in, (((1,), (1,)), ((), ()))...]
    unnamed x6 -> x0, waiting for transfers between devices: 156 us -> none
    all_gather x2 -> x0, waiting for transfers between devices: 120 us -> none  [the longest x1 64.7 us: per_device(): lax.all_gather(tokens, 'tp', axis=0, tiled=True)]
    pallas_call x0 -> x2, Pallas kernels: none -> 98 us  [the longest x1 96.4 us: per_device(): pl.pallas_call(functools.partial(kernel, cfg), out_shape=(jax.ShapeDtypeS...]
    dot_general x5 -> x0, matrix products: 33.2 us -> none  [the longest x1 7.92 us: per_device(): lax.dot_general(act, seq_grad, (((0,), (0,)), ((), ())), preferred_elemen...]
    unnamed x1 -> x6, local copies, waits for them, and re-layouts: 9.65 us -> 2.98 us
  transfers between devices with their start and end apart: 5 -> 0, of which waited for: 5 -> 0; matrix products, arithmetic and copies ran while one was open for 6% -> 0% of each run, Pallas kernels for 0% -> 0%
where the time goes in v2:
time: 103 us; the launch traced here: 102 us
  Pallas kernels  98 us (95%)
  local copies, waits for them, and re-layouts  3.84 us (4%)
    pallas_call x1, Pallas kernels, per_device(): pl.pallas_call(functools.partial(kernel, cfg), out_shape=(jax.ShapeDtypeS...  96.4 us
    unnamed x6, local copies, waits for them, and re-layouts  2.98 us

profile of v2, /device:TPU:1, one launch (start us, length us, event | category | flops | bytes accessed | tf_op | source)
XLA Modules:
  0.0 102.5 jit_solution(6693903269024011632)
XLA Ops:
  0.6 96.4 %shard_map.67 = (bf16[16,18432]{1,0:T(8,128)(2,1)}, f32[576,128]{1,0:T(8,128)}, f32[576,128]{1,0:T(8,128)}) custom-call(bf16[16,18432]{1,0:T(8,128)(2,1)} %tokens.1, bf16[16,18432]{1,0:T(8,128)(2,1)} %upstream.1, bf16[18432,128]{1,0:T(8,128)(2,1)} %w_in.1, bf16[128,18432]{1,0:T(8,128)(2,1)} %w_out.1), custom_call_target="tpu_custom_call" | custom-call | tf_op jit(solution)/shard_map/pallas_call | solution.py:598
  97.0 0.0 copy-start
  97.1 1.1 %copy-done = bf16[16,18432]{1,0:T(8,128)(2,1)S(1)} copy-done((bf16[16,18432]{1,0:T(8,128)(2,1)S(1)}, bf16[16,18432]{1,0:T(8,128)(2,1)}, u32[]{:S(2)}) %copy-start) | copy-done | bytes 589848
  98.1 0.0 copy-start.1
  98.1 1.0 copy-done.1
  99.1 0.0 copy-start.2
  99.1 1.0 copy-done.2
  100.0 1.6 %shard_map.68 = (f32[16,18432]{1,0:T(8,128)}, f32[576,128]{1,0:T(8,128)}, f32[128,576]{1,0:T(8,128)S(1)}) custom-call(bf16[16,18432]{1,0:T(8,128)(2,1)S(1)} %copy-done, f32[576,128]{1,0:T(8,128)S(1)} %copy-done.1, f32[576,128]{1,0:T(8,128)S(1)} %copy-done.2), custom_call_target="tpu_custom_call" | custom-call | tf_op jit(solution)/shard_map/pallas_call | solution.py:612
  101.6 0.9 copy.7
Async XLA Ops:
  97.0 1.1 %copy-start = (bf16[16,18432]{1,0:T(8,128)(2,1)S(1)}, bf16[16,18432]{1,0:T(8,128)(2,1)}, u32[]{:S(2)}) copy-start(bf16[16,18432]{1,0:T(8,128)(2,1)} %get-tuple-element.6.tg) | copy-start | bytes 1769476
  98.1 1.0 copy-start.1
  99.1 1.0 copy-start.2

commit v3 on v2

--- a/solution.py
+++ b/solution.py
@@ -32,6 +32,7 @@
     R = NP * T
     HR = R // 2
     HB = B // 2
+    AP0 = 4 if B % 64 == 0 else 2
     TS = min(256, HID)
     NT = HID // TS
 
@@ -81,8 +82,8 @@
     def landed(ref, sem):
         pltpu.make_async_copy(ref, ref, sem).wait()
 
-    def drain():
-        while sends:
+    def drain(keep=0):
+        while len(sends) > keep:
             sends.pop(0).wait_send()
 
     def slot(m):
@@ -123,37 +124,48 @@
         c_wout.wait()
         w2[pl.ds(row0, B), lanes(0)] = jnp.where(k == 0, wo_tmp[:, 0:B].T, wo_tmp[:, W - B : W].T)
 
-    def part(hf):
-        return pl.ds(mult(row0 + HB * hf, 16), HB)
-
-    def halves(step, d):
-        return (0, 1) if step < H - 1 else (d,)
+    def part(hf, np_=2):
+        return pl.ds(mult(row0 + (B // np_) * hf, 16), B // np_)
+
+    AP = (AP0, 2)
+
+    def ag_parts(wi, step, d):
+        np_ = AP[wi]
+        if step < H - 1:
+            return range(np_)
+        return range(np_ // 2) if d == 0 else range(np_ // 2, np_)
+
+    def ag_sem(wi, step, d, hf):
+        return ((wi * 2 + d) * H + step) * 4 + hf
 
     def ag_send_one(wi, step, d, hf):
         w = (w1, w2)[wi]
         sg = 1 if d else -1
-        n = ((wi * 2 + d) * H + step) * 2 + hf
+        n = ag_sem(wi, step, d, hf)
+        rows = part(hf, AP[wi])
         send(
-            w.at[part(hf), lanes(slot(sg * step))], w.at[part(hf), lanes(slot(sg * (step + 1)))],
+            w.at[rows, lanes(slot(sg * step))], w.at[rows, lanes(slot(sg * (step + 1)))],
             ag_send.at[n], ag_recv.at[n], zn[d],
         )
 
     def ag_start(wi):
-        for hf in (0, 1):
+        for hf in range(AP[wi]):
             for d in (0, 1):
-                if hf in halves(0, d):
+                if hf in ag_parts(wi, 0, d):
                     ag_send_one(wi, 0, d, hf)
 
-    def ag(wi, step, hf):
+    def ag(wi, step, half):
         if step >= H:
             return
         w = (w1, w2)[wi]
-        for d in (0, 1):
-            if hf in halves(step, d):
-                n = ((wi * 2 + d) * H + step) * 2 + hf
-                landed(w.at[part(hf), lanes(slot((1 if d else -1) * (step + 1)))], ag_recv.at[n])
-                if step + 1 < H and hf in halves(step + 1, d):
-                    ag_send_one(wi, step + 1, d, hf)
+        np_ = AP[wi]
+        for hf in range(np_ // 2 * half, np_ // 2 * (half + 1)):
+            for d in (0, 1):
+                if hf in ag_parts(wi, step, d):
+                    n = ag_sem(wi, step, d, hf)
+                    landed(w.at[part(hf, np_), lanes(slot((1 if d else -1) * (step + 1)))], ag_recv.at[n])
+                    if step + 1 < H and hf in ag_parts(wi, step + 1, d):
+                        ag_send_one(wi, step + 1, d, hf)
 
     def a2a_start(src, dst, n, lo, hi):
         @pl.loop(lo, hi)
@@ -180,11 +192,15 @@
     def chunk(c):
         return pl.ds(TS * c, TS)
 
+    def tiles(c):
+        return [pl.ds(TS * c + t, min(256, TS)) for t in range(0, TS, min(256, TS))]
+
     def mm_part(n, c, start):
         lhs, w = ((tokb, w1), (upb, w2))[n]
-        prep[n, pl.ds(start, HR), chunk(c)] = jnp.dot(
-            lhs[pl.ds(start, HR), :], w[:, chunk(c)], preferred_element_type=F32
-        )
+        for cols in tiles(c):
+            prep[n, pl.ds(start, HR), cols] = jnp.dot(
+                lhs[pl.ds(start, HR), :], w[:, cols], preferred_element_type=F32
+            )
 
     def P_(n, c):
         if c >= NT:
@@ -250,7 +266,7 @@
         if (c + 1) % CG == 0:
             GV0(n, c // CG)
 
-    CG = 2 if NT % 2 == 0 else 1
+    CG = 1
     NG = NT // CG
 
     def group(g):
@@ -300,9 +316,8 @@
         @pl.loop(0, 2)
         def _(m):
             rows = pl.ds(mult(MT * m, MT), MT)
-            grad[n, rows, chunk(c)] = jnp.dot(
-                lhsT[rows, :], gath[n, :, chunk(c)], preferred_element_type=F32
-            )
+            for cols in tiles(c):
+                grad[n, rows, cols] = jnp.dot(lhsT[rows, :], gath[n, :, cols], preferred_element_type=F32)
 
     def rs_dest(d, step):
         m = H - step
@@ -401,108 +416,121 @@
     entry_wait()
     ag_start(0)
     a2a_start(tokens, tokb, 0, 1, NP)
+    a2a_start(upstream, upb, 1, 1, NP // 2)
+    a2a_start(upstream, upb, 1, NP // 2, NP)
     own_wout()
+    ag_start(1)
     ag(0, 0, 0)
     ag(0, 0, 1)
-    a2a_start(upstream, upb, 1, 1, NP // 2)
+    ag(1, 0, 0)
     ag(0, 1, 0)
-    ag(0, 1, 1)
     c_tok.wait()
     a2a_wait(tokb, 0, a2a_recv)
     P_(0, 0)
-    ag(0, 2, 0)
+    ag(0, 1, 1)
+    ag(1, 0, 1)
     P_(0, 1)
     S_(0, 0)
+    S_(0, 1)
+    transpose(tokT, tokb)
+    ag(1, 1, 0)
+    ag(0, 2, 0)
     ag(0, 2, 1)
-    ag_start(1)
     P_(0, 2)
-    S_(0, 1)
-    ag(0, 3, 0)
-    ag(0, 3, 1)
-    P_(0, 3)
-    S_(0, 2)
-    U_(0, 0)
-    S_(0, 3)
-    a2a_start(upstream, upb, 1, NP // 2, NP)
-    ag(1, 0, 0)
-    U_(0, 1)
-    V_(0, 0)
-    ag(1, 0, 1)
-    U_(0, 2)
-    V_(0, 1)
-    U_(0, 3)
-    ag(1, 1, 0)
-    V_(0, 2)
-    V_(0, 3)
     ag(1, 1, 1)
-    GV(0, 0)
-    transpose(tokT, tokb)
-    GV(0, 1)
-    ag(1, 2, 0)
-    GU(0, 0)
-    transpose(w1T, w1)
-    ag(1, 2, 1)
-    GU(0, 1)
     c_up.wait()
     a2a_wait(upb, 1, a2a_recv)
+    S_(0, 2)
+    P_(1, 1)
+    ag(1, 2, 0)
+    ag(0, 3, 1)
+    U_(0, 0)
+    U_(0, 1)
+    ag(0, 3, 0)
+    P_(0, 3)
+    S_(1, 1)
     P_(1, 0)
-    P_(1, 1)
+    ag(1, 2, 1)
+    P_(1, 2)
+    ag(1, 3, 1)
+    S_(0, 3)
+    ag(1, 3, 0)
+    P_(1, 3)
+    U_(0, 2)
+    S_(1, 2)
+    S_(1, 3)
+    U_(0, 3)
+    V_(0, 2)
+    S_(1, 0)
+    U_(1, 2)
+    V_(0, 1)
+    V_(0, 0)
+    U_(1, 1)
+    U_(1, 3)
+    V_(0, 3)
+    GV(0, 2)
+    U_(1, 0)
+    V_(1, 2)
+    GV(0, 0)
+    V_(1, 3)
+    GV(0, 3)
+    V_(1, 1)
+    GV(0, 1)
+    transpose(w1T, w1)
+    V_(1, 0)
+    GU(0, 2)
+    GV(1, 2)
+    GV(1, 3)
+    GU(0, 3)
     transpose(upT, upb)
+    GV(1, 1)
+    GS(0, 2)
+    GV(1, 0)
+    GU(0, 1)
+    grad_mm(0, 2)
+    GS(0, 3)
+    grad_mm(0, 3)
+    RS(0, 0)
+    GU(1, 2)
+    GU(1, 3)
+    GU(1, 1)
+    GU(0, 0)
+    GS(1, 2)
+    grad_mm(1, 2)
+    GS(1, 3)
+    grad_mm(1, 3)
+    GS(0, 1)
+    GU(1, 0)
+    RS(1, 0)
+    RS(0, 1)
+    GS(1, 1)
     GS(0, 0)
+    GS(1, 0)
+    tg_mm(0, 4)
+    tg_start()
+    RS(1, 1)
+    grad_mm(0, 1)
+    grad_mm(1, 0)
     grad_mm(0, 0)
-    grad_mm(0, 1)
-    S_(1, 0)
-    P_(1, 2)
-    GS(0, 1)
-    grad_mm(0, 3)
-    grad_mm(0, 2)
-    RS(0, 0)
-    S_(1, 1)
-    ag(1, 3, 0)
-    ag(1, 3, 1)
-    P_(1, 3)
-    S_(1, 2)
-    U_(1, 0)
-    S_(1, 3)
-    U_(1, 1)
-    V_(1, 0)
-    RS(0, 1)
-    U_(1, 2)
-    V_(1, 1)
-    U_(1, 3)
-    V_(1, 2)
-    V_(1, 3)
-    GV(1, 0)
+    drain(40)
     RS(0, 2)
-    GV(1, 1)
-    GU(1, 0)
+    grad_mm(1, 1)
+    drain(40)
+    RS(1, 2)
     RS(0, 3)
-    GU(1, 1)
-    GS(1, 0)
-    GS(1, 1)
-    for c in range(NT - 1, max(NT - 3, -1), -1):
-        grad_mm(1, c)
-    RS(1, 0)
-    for c in range(NT - 2):
-        grad_mm(1, c)
-    tg_mm(0, 2)
-    RS(1, 1)
-    tg_mm(2, 4)
-    tg_start()
+    drain(40)
+    RS(1, 3)
     RS_end(0)
     c_o = pltpu.make_async_copy(res.at[0], outg_out, loc_sem.at[0])
     c_o.start()
-    RS(1, 2)
-    drain()
-    a2a_wait(tokb, 0, a2a_send)
-    a2a_wait(upb, 1, a2a_send)
-    RS(1, 3)
     tg_end()
     c_t = pltpu.make_async_copy(tga, tg_out, loc_sem.at[1])
     c_t.start()
     RS_end(1)
     c_i = pltpu.make_async_copy(res.at[1], ing_out, loc_sem.at[2])
     c_i.start()
+    a2a_wait(tokb, 0, a2a_send)
+    a2a_wait(upb, 1, a2a_send)
     drain()
     a2a_wait(tgb, 2, a2a_send)
     c_o.wait()
@@ -510,11 +538,11 @@
     c_i.wait()
 
 
-def finish(tg, ing, outg, tg_o, ing_o, outg_o, tb, tf, ob, ot, sem):
+def finish(tg, ing, outg, tg_o, ing_o, outg_o, tb, tf, sem):
     NC = 4
     D = tb.shape[1]
     C = D // NC
-    c_o = pltpu.make_async_copy(outg, ob, sem.at[0])
+    c_o = pltpu.make_async_copy(outg, outg_o, sem.at[0])
     c_o.start()
     c_i = pltpu.make_async_copy(ing, ing_o, sem.at[1])
     c_i.start()
@@ -530,10 +558,6 @@
         o.start()
         outs.append(o)
     c_o.wait()
-    ot[...] = ob[...].T
-    o = pltpu.make_async_copy(ot, outg_o, sem.at[2 + 2 * NC])
-    o.start()
-    outs.append(o)
     c_i.wait()
     for o in outs:
         o.wait()
@@ -584,8 +608,8 @@
             DMA((4,)),
             DMA((3,)),
             DMA((3,)),
-            DMA((8 * H,)),
-            DMA((8 * H,)),
+            DMA((16 * H,)),
+            DMA((16 * H,)),
             DMA((8 * H,)),
             DMA((8 * H,)),
             DMA((NQ,)),
@@ -602,31 +626,30 @@
                 jax.ShapeDtypeStruct((B, 128), F32),
                 jax.ShapeDtypeStruct((B, 128), F32),
             ),
-            in_specs=[pl.BlockSpec(memory_space=pl.ANY)] * 4,
+            in_specs=[pl.BlockSpec(memory_space=pltpu.HBM)] * 4,
             out_specs=tuple([pl.BlockSpec(memory_space=pl.ANY)] * 3),
             scratch_shapes=scratch,
             compiler_params=pltpu.CompilerParams(
-                collective_id=0, has_side_effects=True, vmem_limit_bytes=56 * 2**20
+                collective_id=0, has_side_effects=True, vmem_limit_bytes=105 * 2**19
             ),
         )(tokens, upstream, w_in, w_out)
-        return pl.pallas_call(
+        tg_f, ing_f, outg_f = pl.pallas_call(
             finish,
             out_shape=(
                 jax.ShapeDtypeStruct((T, D), F32),
                 jax.ShapeDtypeStruct((B, 128), F32),
-                jax.ShapeDtypeStruct((128, B), F32),
+                jax.ShapeDtypeStruct((B, 128), F32),
             ),
             in_specs=[pl.BlockSpec(memory_space=pl.ANY)] * 3,
             out_specs=tuple([pl.BlockSpec(memory_space=pl.ANY)] * 3),
             scratch_shapes=[
                 pltpu.VMEM((T, D), BF16),
                 pltpu.VMEM((T, D), F32),
-                pltpu.VMEM((B, 128), F32),
-                pltpu.VMEM((128, B), F32),
-                DMA((11,)),
+                DMA((10,)),
             ],
-            compiler_params=pltpu.CompilerParams(vmem_limit_bytes=16 * 2**20),
+            compiler_params=pltpu.CompilerParams(vmem_limit_bytes=50 * 2**20),
         )(tg, ing, outg)
+        return tg_f, ing_f, outg_f.T
 
     return per_device
 

time: 103 us -> 90.8 us (0.88)
  Pallas kernels: 98 us -> 90 us
  local copies, waits for them, and re-layouts: 3.84 us -> 0 us
    pallas_call x1, Pallas kernels: 96.4 us -> 88.5 us  [per_device(): pl.pallas_call(functools.partial(kernel, cfg), out_shape=(jax.ShapeDtypeS...]
    unnamed x6 -> x0, local copies, waits for them, and re-layouts: 2.98 us -> none
where the time goes in v3:
time: 90.8 us; the launch traced here: 90.7 us
  Pallas kernels  90 us (99%)
    pallas_call x1, Pallas kernels, per_device(): pl.pallas_call(functools.partial(kernel, cfg), out_shape=(jax.ShapeDtypeS...  88.5 us

profile of v3, /device:TPU:1, one launch (start us, length us, event | category | flops | bytes accessed | tf_op | source)
XLA Modules:
  0.0 90.7 jit_solution(11579958810899393659)
XLA Ops:
  0.6 88.5 %shard_map.67 = (bf16[16,18432]{1,0:T(8,128)(2,1)S(1)}, f32[576,128]{1,0:T(8,128)S(1)}, f32[576,128]{1,0:T(8,128)S(1)}) custom-call(bf16[16,18432]{1,0:T(8,128)(2,1)} %tokens.1, bf16[16,18432]{1,0:T(8,128)(2,1)} %upstream.1, bf16[18432,128]{1,0:T(8,128)(2,1)} %w_in.1, bf16[128,18432]{1,0:T(8,128)(2,1)} %w_out.1), custom_call_target="tpu_custom_call" | custom-call | tf_op jit(solution)/shard_map/pallas_call | solution.py:622
  89.2 1.5 %shard_map.68 = (f32[16,18432]{1,0:T(8,128)}, f32[576,128]{1,0:T(8,128)}, f32[576,128]{1,0:T(8,128)}) custom-call(bf16[16,18432]{1,0:T(8,128)(2,1)S(1)} %get-tuple-element.9.tg, f32[576,128]{1,0:T(8,128)S(1)} %get-tuple-element.10.ing, f32[576,128]{1,0:T(8,128)S(1)} %get-tuple-element.11.outg), custom_call_target="tpu_custom_call" | custom-call | tf_op jit(solution)/shard_map/pallas_call | solution.py:636

commit v4 on v0

v4 whole, which is shorter than its diff:
```python
import functools

import jax
import jax.numpy as jnp
from jax import lax
from jax.experimental import pallas as pl
from jax.experimental.pallas import tpu as pltpu
from jax.sharding import PartitionSpec as P

MESH = pl.DeviceIdType.MESH
F32 = jnp.float32
BF16 = jnp.bfloat16


def mult(value, of):
    return pl.multiple_of(value, of)


def kernel(
    cfg,
    tokens, upstream, w_in, w_out,
    tg_out, ing_out, outg_out,
    tokb, upb, tokT, upT, own1, own2, w1, w2, w1T, wo_tmp,
    prep, urecv, usum, vrecv, pos, gath,
    grad, ownp, zsend, zrecv, zfin, tgp, tgx, tgb, res,
    loc_sem, a2a_send, a2a_recv, f_send, f_recv, ag_sent, ag_recv, rs_sent, rs_recv,
    fin_sent, fin_recv, u_send, u_recv, v_send, v_recv,
):
    NXL, NDP, NZ, NS, T, B = cfg
    NP = NXL * NDP
    NC = NP // 2
    H = NZ // 2
    BC = 2 * B
    R = NP * T
    RC = R // 2
    UR = R // NS
    VR = UR // NS
    HP = B // 2

    z = lax.axis_index("tp")
    dcn = lax.axis_index("dcn")
    dp = lax.axis_index("dp")
    k = dp % 2
    y = (dp // 2) % NS
    x = (dp // (2 * NS)) * NXL + dcn
    p = (dcn * NDP + dp) // 2
    u = jnp.where(k == 0, x, y)
    v = jnp.where(k == 0, y, x)
    up = (z + 1) % NZ
    down = (z + NZ - 1) % NZ

    def dev(x_, y_, k_):
        return (x_ % NXL, (x_ // NXL) * (2 * NS) + y_ * 2 + k_, z)

    def chip(p_):
        i_ = 2 * p_ + k
        return (i_ // NDP, i_ % NDP, z)

    def at_z(z_, k_):
        return (dcn, dp - k + k_, z_)

    sib = dev(x, y, 1 - k)

    def u_peer(u_):
        return dev(jnp.where(k == 0, u_, x), jnp.where(k == 0, y, u_), k)

    def v_peer(v_):
        return dev(jnp.where(k == 0, x, v_), jnp.where(k == 0, v_, y), k)

    ag_z = jnp.where(k == 0, up, down)
    rs_z = jnp.where(k == 0, down, up)

    sends = []

    def send(src, dst, ss, rs, to, when=None):
        c = pltpu.make_async_remote_copy(
            src_ref=src, dst_ref=dst, send_sem=ss, recv_sem=rs, device_id=to, device_id_type=MESH
        )
        if when is None:
            c.start()
        else:
            pl.when(when)(c.start)
        sends.append((when, c))
        return c

    def landed(ref, sem):
        pltpu.make_async_copy(ref, ref, sem).wait()

    def drain(keep=0):
        while len(sends) > keep:
            when, c = sends.pop(0)
            if when is None:
                c.wait_send()
            else:
                pl.when(when)(c.wait_send)

    LAST = H - 1

    def lanes(c, n=1):
        return pl.ds(128 * c, 128 * n)

    barrier = pltpu.get_barrier_semaphore()
    cols = pl.ds(mult(BC * p, 128), BC)
    my_tok = pl.ds(mult(RC * k + T * p, T), T)
    my_half = pl.ds(mult(RC * k, RC), RC)
    sib_half = pl.ds(mult(RC * (1 - k), RC), RC)

    def entry():
        for z_ in (up, down) if NZ > 2 else (up,):
            for k_ in (0, 1):
                pl.semaphore_signal(barrier, inc=1, device_id=at_z(z_, k_), device_id_type=MESH)
        pl.semaphore_signal(barrier, inc=1, device_id=sib, device_id_type=MESH)

        @pl.loop(1, NC)
        def _(d):
            pl.semaphore_signal(barrier, inc=1, device_id=chip((p + d) % NC), device_id_type=MESH)

    c_win = pltpu.make_async_copy(w_in.at[pl.ds(mult(BC * p, 128), BC), :], own1, loc_sem.at[0])
    c_wout = pltpu.make_async_copy(w_out.at[:, cols], wo_tmp, loc_sem.at[1])
    c_tok = pltpu.make_async_copy(tokens.at[:, cols], tokb.at[my_tok, :], loc_sem.at[2])
    c_up = pltpu.make_async_copy(upstream.at[:, cols], upb.at[my_tok, :], loc_sem.at[3])

    def entry_wait():
        c_win.wait()
        pl.semaphore_wait(barrier, NC + (4 if NZ > 2 else 2))

    def own_wout():
        c_wout.wait()
        own2[...] = wo_tmp[...].T

        @pl.when(k == 0)
        def _():
            w1[:, lanes(LAST)] = own1[...]
            w2[:, lanes(LAST)] = own2[...]

    def rows_at(q):
        return pl.ds(HP * q, HP)

    def ag_block(wi, step):
        return (own1, own2)[wi] if step == 0 else (w1, w2)[wi].at[:, lanes(step - 1)]

    def ag_sem(wi, step, q):
        return (wi * H + step) * 4 + q

    def ag_send(wi, step, q):
        w = (w1, w2)[wi]
        n = ag_sem(wi, step, q)
        src = ag_block(wi, step).at[rows_at(q), :]
        if step < H - 1:
            send(src, w.at[rows_at(q), lanes(step)], ag_sent.at[n], ag_recv.at[n], at_z(ag_z, k))
        else:
            send(
                src, w.at[rows_at(q), lanes(LAST)], ag_sent.at[n], ag_recv.at[n], at_z(ag_z, 1),
                when=k == q // 2,
            )


    def ag_start(wi):
        for q in range(4):
            ag_send(wi, 0, q)

    def ag(wi, step, half):
        w = (w1, w2)[wi]
        for q in (2 * half, 2 * half + 1):
            arrived = w.at[rows_at(q), lanes(step)]
            if step < H - 1:
                landed(arrived, ag_recv.at[ag_sem(wi, step, q)])
                ag_send(wi, step + 1, q)
            else:
                pl.when(k == 1)(functools.partial(landed, arrived, ag_recv.at[ag_sem(wi, step, q)]))

    def a2a_start(src, dst, n):
        @pl.loop(1, NC)
        def _(d):
            to = (p + d) % NC
            pltpu.make_async_remote_copy(
                src_ref=src.at[:, pl.ds(mult(BC * to, 128), BC)],
                dst_ref=dst.at[my_tok, :],
                send_sem=a2a_send.at[n],
                recv_sem=a2a_recv.at[n],
                device_id=chip(to),
                device_id_type=MESH,
            ).start()

    def a2a_wait(n, sems):
        landed(tokb.at[pl.ds(0, RC - T), :], sems.at[n])

    def A2F(n):
        (c_tok, c_up)[n].wait()
        a2a_wait(n, a2a_recv)
        ref = (tokb, upb)[n].at[my_half, :]
        send(ref, ref, f_send.at[n], f_recv.at[n], sib)

    def A2W(n):
        landed((tokb, upb)[n].at[sib_half, :], f_recv.at[n])

    mine = pl.ds(mult(UR * u + VR * v, VR), VR)
    u_rows = pl.ds(mult(UR * u, UR), UR)
    pend = {}

    def P_(n, c, count):
        lhs, w = ((tokb, w1), (upb, w2))[n]
        prep[n, :, lanes(c, count)] = jnp.dot(lhs[...], w[:, lanes(c, count)], preferred_element_type=F32)

    def S_(n, c):
        q = n * H + c
        out = []
        for r in [2, 1, 3] if NS == 4 else range(1, NS):
            uu = (u + r) % NS
            out.append(
                send(
                    prep.at[n, pl.ds(mult(UR * uu, UR), UR), lanes(c)], urecv.at[n, r - 1, :, lanes(c)],
                    u_send.at[q, r - 1], u_recv.at[q, r - 1], u_peer(uu),
                )
            )
        pend["u", n, c] = out

    def U_(n, c):
        q = n * H + c
        for d in pend["u", n, c]:
            d.wait_recv()
        tot = prep[n, u_rows, lanes(c)]
        for r in range(NS - 1):
            tot = tot + urecv[n, r, :, lanes(c)]
        usum[n, :, lanes(c)] = tot
        pend["v", n, c] = [
            send(
                usum.at[n, pl.ds(mult(VR * ((v + r) % NS), VR), VR), lanes(c)], vrecv.at[n, r - 1, :, lanes(c)],
                v_send.at[q, r - 1], v_recv.at[q, r - 1], v_peer((v + r) % NS),
            )
            for r in range(1, NS)
        ]

    def V_(n, c):
        q = 2 * H + n * H + c
        for d in pend["v", n, c]:
            d.wait_recv()
        tot = usum[n, pl.ds(mult(VR * v, VR), VR), lanes(c)]
        for r in range(NS - 1):
            tot = tot + vrecv[n, r, :, lanes(c)]
        if n == 0:
            positive = jnp.maximum(tot, 0.0)
            pos[:, lanes(c)] = positive
            gath[0, mine, lanes(c)] = (positive * positive).astype(BF16)
        else:
            gath[1, mine, lanes(c)] = (tot * 2.0 * pos[:, lanes(c)]).astype(BF16)
        ref = gath.at[n, mine, lanes(c)]
        pend["gv", n, c] = [
            send(ref, ref, v_send.at[q, r - 1], v_recv.at[q, r - 1], v_peer((v + r) % NS)) for r in range(1, NS)
        ]

    def GV(n, c):
        q = 2 * H + n * H + c
        for d in pend["gv", n, c]:
            d.wait_recv()
        ref = gath.at[n, u_rows, lanes(c)]
        pend["gu", n, c] = [
            send(ref, ref, u_send.at[q, r - 1], u_recv.at[q, r - 1], u_peer((u + r) % NS)) for r in range(1, NS)
        ]

    def GU(n, c):
        for d in pend["gu", n, c]:
            d.wait_recv()

    def grad_mm(n, c, count):
        lhsT = (upT, tokT)[n]
        grad[n, :, lanes(c, count)] = jnp.dot(lhsT[...], gath[n, :, lanes(c, count)], preferred_element_type=F32)

    def half_rows(hf):
        return pl.ds(mult(B * hf, 64), B)

    def rs_one(n, step, hf, recv):
        q = n * H + step
        rows = half_rows(hf)
        val = grad[n, rows, lanes(H - 1 - step)]
        if recv:
            landed(zrecv.at[q - 1, rows, :], rs_recv.at[2 * (q - 1) + hf])
            val = val + zrecv[q - 1, rows, :].astype(F32)
        zsend[q, rows, :] = val.astype(BF16)
        if step < H - 1:
            send(
                zsend.at[q, rows, :], zrecv.at[q, rows, :], rs_sent.at[2 * q + hf], rs_recv.at[2 * q + hf],
                at_z(rs_z, k),
            )
        else:
            send(zsend.at[q, rows, :], zfin.at[n, k], fin_sent.at[2 * n + hf], fin_recv.at[2 * n + k], at_z(rs_z, hf))

    def RS(n, step):
        if step == 0:
            q = n * H

            @pl.when(k == 1)
            def _():
                zsend[q] = grad[n, :, lanes(LAST)].astype(BF16)

            for hf, to in ((0, at_z(up, 1)), (1, at_z(down, 0))):
                rows = pl.ds(B * hf, B)
                send(
                    zsend.at[q, rows, :], zrecv.at[q, rows, :], rs_sent.at[2 * q + hf], rs_recv.at[2 * q + hf], to,
                    when=k == 1,
                )
            rs_one(n, 1, k, False)
            send(
                grad.at[n, pl.ds(B, B), lanes(LAST)], ownp.at[n], f_send.at[2 + n], f_recv.at[2 + n], sib, when=k == 0
            )
        elif step == 1:
            rs_one(n, 1, 1 - k, True)
        else:
            rs_one(n, step, k, True)
            rs_one(n, step, 1 - k, True)

    def RS_end(n):
        for d in (0, 1):
            landed(zfin.at[n, d], fin_recv.at[2 * n + d])
        tot = zfin[n, 0].astype(F32) + zfin[n, 1].astype(F32)

        @pl.when(k == 0)
        def _():
            res[n] = tot + grad[n, 0:B, lanes(LAST)]

        @pl.when(k == 1)
        def _():
            landed(ownp.at[n], f_recv.at[2 + n])
            res[n] = tot + ownp[n]

    TR = min(128, RC)

    def tg_mm(half):
        @pl.loop(0, RC // TR)
        def _(t):
            rows = pl.ds(mult(RC * half + TR * t, TR), TR)
            tgp[rows, :] = jnp.dot(gath[1, rows, :], w1T[...], preferred_element_type=F32)

    def TG():
        tg_mm(1 - k)
        send(tgp.at[sib_half, :], tgx, f_send.at[4], f_recv.at[4], sib)
        tg_mm(k)

    c_t = pltpu.make_async_copy(tgb.at[pl.ds(mult(T * p, T), T), :], tg_out.at[:, cols], loc_sem.at[4])

    def TG2():
        landed(tgx, f_recv.at[4])

        @pl.loop(0, RC // TR)
        def _(t):
            rows = pl.ds(mult(TR * t, TR), TR)
            tgb[rows, :] = (tgp[pl.ds(mult(RC * k + TR * t, TR), TR), :] + tgx[rows, :]).astype(BF16)

        @pl.loop(1, NC)
        def _(d):
            to = (p + d) % NC
            pltpu.make_async_remote_copy(
                src_ref=tgb.at[pl.ds(mult(T * to, T), T), :],
                dst_ref=tg_out.at[:, cols],
                send_sem=a2a_send.at[2],
                recv_sem=a2a_recv.at[2],
                device_id=chip(to),
                device_id_type=MESH,
            ).start()

        c_t.start()

    def TGE():
        landed(tg_out.at[:, pl.ds(0, BC * (NC - 1))], a2a_recv.at[2])
        c_t.wait()

    def transpose(dst, src):
        dst[...] = src[...].T

    entry()
    for c in (c_win, c_wout, c_tok, c_up):
        c.start()
    entry_wait()
    ag_start(0)
    own_wout()
    a2a_start(tokens, tokb, 0)
    ag_start(1)
    a2a_start(upstream, upb, 1)
    ag(0, 0, 0)
    ag(0, 0, 1)
    ag(1, 0, 0)
    ag(0, 1, 0)
    ag(1, 0, 1)
    A2F(0)
    ag(0, 1, 1)
    ag(1, 1, 0)
    A2W(0)
    P_(0, 1, 1)
    ag(1, 1, 1)
    ag(0, 2, 0)
    P_(0, 0, 1)
    A2F(1)
    S_(0, 1)
    ag(0, 2, 1)
    P_(0, 2, 1)
    S_(0, 0)
    ag(1, 2, 0)
    S_(0, 2)
    ag(1, 2, 1)
    A2W(1)
    P_(1, 2, 1)
    S_(1, 2)
    ag(0, 3, 1)
    ag(0, 3, 0)
    P_(0, 3, 1)
    S_(0, 3)
    P_(1, 0, 2)
    ag(1, 3, 0)
    transpose(upT, upb)
    S_(1, 0)
    ag(1, 3, 1)
    P_(1, 3, 1)
    U_(0, 2)
    S_(1, 3)
    U_(1, 2)
    U_(0, 3)
    U_(0, 0)
    S_(1, 1)
    V_(0, 2)
    U_(0, 1)
    U_(1, 3)
    U_(1, 0)
    V_(0, 3)
    V_(1, 2)
    V_(0, 0)
    U_(1, 1)
    GV(0, 2)
    V_(0, 1)
    V_(1, 3)
    V_(1, 0)
    GV(0, 3)
    GV(1, 2)
    V_(1, 1)
    GV(1, 3)
    GU(0, 2)
    transpose(tokT, tokb)
    GV(0, 1)
    grad_mm(0, 2, 1)
    GU(0, 3)
    grad_mm(0, 3, 1)
    RS(0, 0)
    GU(1, 2)
    GV(1, 0)
    GV(0, 0)
    GV(1, 1)
    grad_mm(1, 2, 1)
    GU(1, 3)
    grad_mm(1, 3, 1)
    RS(1, 0)
    transpose(w1T, w1)
    GU(0, 1)
    GU(0, 0)
    RS(0, 1)
    GU(1, 0)
    GU(1, 1)
    TG()
    RS(1, 1)
    grad_mm(1, 1, 1)
    grad_mm(0, 1, 1)
    drain(40)
    RS(0, 2)
    grad_mm(0, 0, 1)
    grad_mm(1, 0, 1)
    drain(40)
    RS(1, 2)
    TG2()
    RS(0, 3)
    drain(40)
    RS(1, 3)
    RS_end(0)
    c_o = pltpu.make_async_copy(res.at[0], outg_out, loc_sem.at[0])
    c_o.start()
    TGE()
    RS_end(1)
    c_i = pltpu.make_async_copy(res.at[1], ing_out, loc_sem.at[2])
    c_i.start()
    drain()
    for n in range(3):
        a2a_wait(n, a2a_send)
    c_o.wait()
    c_i.wait()


def finish(tg, ing, outg, tg_o, ing_o, outg_o, tb, tf, sem):
    NC = 4
    D = tb.shape[1]
    C = D // NC
    c_o = pltpu.make_async_copy(outg, outg_o, sem.at[0])
    c_o.start()
    c_i = pltpu.make_async_copy(ing, ing_o, sem.at[1])
    c_i.start()
    ins = [pltpu.make_async_copy(tg.at[:, pl.ds(C * c, C)], tb.at[:, pl.ds(C * c, C)], sem.at[2 + c]) for c in range(NC)]
    for c in ins:
        c.start()
    outs = []
    for n in range(NC):
        ins[n].wait()
        cols = pl.ds(C * n, C)
        tf[:, cols] = tb[:, cols].astype(F32)
        o = pltpu.make_async_copy(tf.at[:, cols], tg_o.at[:, cols], sem.at[2 + NC + n])
        o.start()
        outs.append(o)
    c_o.wait()
    c_i.wait()
    for o in outs:
        o.wait()


def make(mesh):
    NXL, NDP, NZ = mesh.shape["dcn"], mesh.shape["dp"], mesh.shape["tp"]
    NP = NXL * NDP
    NS = 1
    while NS * NS * 2 < NP:
        NS += 1

    def per_device(tokens, upstream, w_in, w_out):
        T, D = tokens.shape
        B = D // NP
        BC = 2 * B
        H = NZ // 2
        HL = 128 * H
        R = NP * T
        RC = R // 2
        UR = R // NS
        VR = UR // NS
        cfg = (NXL, NDP, NZ, NS, T, B)
        DMA = pltpu.SemaphoreType.DMA
        VM = pltpu.VMEM
        scratch = [
            VM((R, BC), BF16),
            VM((R, BC), BF16),
            VM((BC, R), BF16),
            VM((BC, R), BF16),
            VM((BC, 128), BF16),
            VM((BC, 128), BF16),
            VM((BC, HL), BF16),
            VM((BC, HL), BF16),
            VM((HL, BC), BF16),
            VM((128, BC), BF16),
            VM((2, R, HL), F32),
            VM((2, NS - 1, UR, HL), F32),
            VM((2, UR, HL), F32),
            VM((2, NS - 1, VR, HL), F32),
            VM((VR, HL), F32),
            VM((2, R, HL), BF16),
            VM((2, BC, HL), F32),
            VM((2, B, 128), F32),
            VM((2 * H, BC, 128), BF16),
            VM((2 * H, BC, 128), BF16),
            VM((2, 2, B, 128), BF16),
            VM((R, BC), F32),
            VM((RC, BC), F32),
            VM((RC, BC), BF16),
            VM((2, B, 128), F32),
            DMA((5,)),
            DMA((3,)),
            DMA((3,)),
            DMA((5,)),
            DMA((5,)),
            DMA((8 * H,)),
            DMA((8 * H,)),
            DMA((4 * H,)),
            DMA((4 * H,)),
            DMA((4,)),
            DMA((4,)),
            DMA((4 * H, NS - 1)),
            DMA((4 * H, NS - 1)),
            DMA((4 * H, NS - 1)),
            DMA((4 * H, NS - 1)),
        ]
        tg, ing, outg = pl.pallas_call(
            functools.partial(kernel, cfg),
            out_shape=(
                jax.ShapeDtypeStruct((T, D), BF16),
                jax.ShapeDtypeStruct((B, 128), F32),
                jax.ShapeDtypeStruct((B, 128), F32),
            ),
            in_specs=[pl.BlockSpec(memory_space=pl.ANY)] * 4,
            out_specs=tuple([pl.BlockSpec(memory_space=pl.ANY)] * 3),
            scratch_shapes=scratch,
            compiler_params=pltpu.CompilerParams(
                collective_id=0, has_side_effects=True, vmem_limit_bytes=105 * 2**19
            ),
        )(tokens, upstream, w_in, w_out)
        tg_f, ing_f, outg_f = pl.pallas_call(
            finish,
            out_shape=(
                jax.ShapeDtypeStruct((T, D), F32),
                jax.ShapeDtypeStruct((B, 128), F32),
                jax.ShapeDtypeStruct((B, 128), F32),
            ),
            in_specs=[pl.BlockSpec(memory_space=pl.ANY)] * 3,
            out_specs=tuple([pl.BlockSpec(memory_space=pl.ANY)] * 3),
            scratch_shapes=[
                pltpu.VMEM((T, D), BF16),
                pltpu.VMEM((T, D), F32),
                DMA((10,)),
            ],
            compiler_params=pltpu.CompilerParams(vmem_limit_bytes=50 * 2**20),
        )(tg, ing, outg)
        return tg_f, ing_f, outg_f.T

    return per_device


def solution(mesh):
    placed = (
        P(("dcn", "dp", "tp"), None),
        P(("dcn", "dp", "tp"), None),
        P(None, "tp"),
        P("tp", None),
    )
    return jax.shard_map(
        make(mesh),
        mesh=mesh,
        in_specs=placed,
        out_specs=(P(("dcn", "dp", "tp"), None), P(("dcn", "dp"), "tp"), P("tp", ("dcn", "dp"))),
        check_vma=False,
    )
```

time: 561 us -> 81.2 us (0.14)
  waiting for transfers between devices: 504 us -> 0 us
  Pallas kernels: 0 us -> 80.4 us
  matrix products: 33.2 us -> 0 us
  between operations: 13.8 us -> 0.64 us
  local copies, waits for them, and re-layouts: 9.65 us -> 0 us
    reduce_scatter x2 -> x0, waiting for transfers between devices: 228 us -> none  [the longest x1 115 us: per_device(): lax.psum_scatter(lax.dot_general(pre_grad, w_in, (((1,), (1,)), ((), ()))...]
    unnamed x6 -> x0, waiting for transfers between devices: 156 us -> none
    all_gather x2 -> x0, waiting for transfers between devices: 120 us -> none  [the longest x1 64.7 us: per_device(): lax.all_gather(tokens, 'tp', axis=0, tiled=True)]
    pallas_call x0 -> x2, Pallas kernels: none -> 80.4 us  [the longest x1 78.9 us: per_device(): pl.pallas_call(functools.partial(kernel, cfg), out_shape=(jax.ShapeDtypeS...]
    dot_general x5 -> x0, matrix products: 33.2 us -> none  [the longest x1 7.92 us: per_device(): lax.dot_general(act, seq_grad, (((0,), (0,)), ((), ())), preferred_elemen...]
    unnamed x1 -> x0, local copies, waits for them, and re-layouts: 9.65 us -> none
  transfers between devices with their start and end apart: 5 -> 0, of which waited for: 5 -> 0; matrix products, arithmetic and copies ran while one was open for 6% -> 0% of each run, Pallas kernels for 0% -> 0%
where the time goes in v4:
time: 81.2 us; the launch traced here: 81.1 us
  Pallas kernels  80.4 us (99%)
    pallas_call x1, Pallas kernels, per_device(): pl.pallas_call(functools.partial(kernel, cfg), out_shape=(jax.ShapeDtypeS...  78.9 us

profile of v4, /device:TPU:1, one launch (start us, length us, event | category | flops | bytes accessed | tf_op | source)
XLA Modules:
  0.0 81.1 jit_solution(1733437051508294898)
XLA Ops:
  0.6 78.9 %shard_map.67 = (bf16[16,18432]{1,0:T(8,128)(2,1)S(1)}, f32[576,128]{1,0:T(8,128)S(1)}, f32[576,128]{1,0:T(8,128)S(1)}) custom-call(bf16[16,18432]{1,0:T(8,128)(2,1)} %tokens.1, bf16[16,18432]{1,0:T(8,128)(2,1)} %upstream.1, bf16[18432,128]{1,0:T(8,128)(2,1)} %w_in.1, bf16[128,18432]{1,0:T(8,128)(2,1)} %w_out.1), custom_call_target="tpu_custom_call" | custom-call | tf_op jit(solution)/shard_map/pallas_call | solution.py:571
  79.6 1.5 %shard_map.68 = (f32[16,18432]{1,0:T(8,128)}, f32[576,128]{1,0:T(8,128)}, f32[576,128]{1,0:T(8,128)}) custom-call(bf16[16,18432]{1,0:T(8,128)(2,1)S(1)} %get-tuple-element.9.tg, f32[576,128]{1,0:T(8,128)S(1)} %get-tuple-element.10.ing, f32[576,128]{1,0:T(8,128)S(1)} %get-tuple-element.11.outg), custom_call_target="tpu_custom_call" | custom-call | tf_op jit(solution)/shard_map/pallas_call | solution.py:585

commit v5 on v4

--- a/solution.py
+++ b/solution.py
@@ -21,10 +21,10 @@
     tokens, upstream, w_in, w_out,
     tg_out, ing_out, outg_out,
     tokb, upb, tokT, upT, own1, own2, w1, w2, w1T, wo_tmp,
-    prep, urecv, usum, vrecv, pos, gath,
-    grad, ownp, zsend, zrecv, zfin, tgp, tgx, tgb, res,
+    prep, urecv, usum, vrecv, vv, pos, posv, gath,
+    grad, ownp, zsend, zrecv, zfin, tgp, tgx, tgb,
     loc_sem, a2a_send, a2a_recv, f_send, f_recv, ag_sent, ag_recv, rs_sent, rs_recv,
-    fin_sent, fin_recv, u_send, u_recv, v_send, v_recv,
+    fin_recv, u_send, u_recv, v_send, v_recv,
 ):
     NXL, NDP, NZ, NS, T, B = cfg
     NP = NXL * NDP
@@ -121,10 +121,10 @@
     c_up = pltpu.make_async_copy(upstream.at[:, cols], upb.at[my_tok, :], loc_sem.at[3])
 
     def entry_wait():
+        pl.semaphore_wait(barrier, NC + (4 if NZ > 2 else 2))
+
+    def own_wout():
         c_win.wait()
-        pl.semaphore_wait(barrier, NC + (4 if NZ > 2 else 2))
-
-    def own_wout():
         c_wout.wait()
         own2[...] = wo_tmp[...].T
 
@@ -145,7 +145,10 @@
     def ag_send(wi, step, q):
         w = (w1, w2)[wi]
         n = ag_sem(wi, step, q)
-        src = ag_block(wi, step).at[rows_at(q), :]
+        if wi == 0 and step == 0:
+            src = w_in.at[pl.ds(mult(BC * p + HP * q, 32), HP), :]
+        else:
+            src = ag_block(wi, step).at[rows_at(q), :]
         if step < H - 1:
             send(src, w.at[rows_at(q), lanes(step)], ag_sent.at[n], ag_recv.at[n], at_z(ag_z, k))
         else:
@@ -223,6 +226,14 @@
         for r in range(NS - 1):
             tot = tot + urecv[n, r, :, lanes(c)]
         usum[n, :, lanes(c)] = tot
+        if c == -1:
+            vv[n, v] = tot
+            mine_all = usum.at[n, :, lanes(c)]
+            pend["v", n, c] = [
+                send(mine_all, vv.at[n, v], v_send.at[q, r - 1], v_recv.at[q, r - 1], v_peer((v + r) % NS))
+                for r in range(1, NS)
+            ]
+            return
         pend["v", n, c] = [
             send(
                 usum.at[n, pl.ds(mult(VR * ((v + r) % NS), VR), VR), lanes(c)], vrecv.at[n, r - 1, :, lanes(c)],
@@ -235,6 +246,17 @@
         q = 2 * H + n * H + c
         for d in pend["v", n, c]:
             d.wait_recv()
+        if c == -1:
+            tot = vv[n, 0]
+            for r in range(1, NS):
+                tot = tot + vv[n, r]
+            if n == 0:
+                positive = jnp.maximum(tot, 0.0)
+                posv[...] = positive
+                gath[0, u_rows, lanes(c)] = (positive * positive).astype(BF16)
+            else:
+                gath[1, u_rows, lanes(c)] = (tot * 2.0 * posv[...]).astype(BF16)
+            return
         tot = usum[n, pl.ds(mult(VR * v, VR), VR), lanes(c)]
         for r in range(NS - 1):
             tot = tot + vrecv[n, r, :, lanes(c)]
@@ -251,8 +273,9 @@
 
     def GV(n, c):
         q = 2 * H + n * H + c
-        for d in pend["gv", n, c]:
-            d.wait_recv()
+        if c != -1:
+            for d in pend["gv", n, c]:
+                d.wait_recv()
         ref = gath.at[n, u_rows, lanes(c)]
         pend["gu", n, c] = [
             send(ref, ref, u_send.at[q, r - 1], u_recv.at[q, r - 1], u_peer((u + r) % NS)) for r in range(1, NS)
@@ -271,19 +294,20 @@
 
     def rs_one(n, step, hf, recv):
         q = n * H + step
-        rows = half_rows(hf)
-        val = grad[n, rows, lanes(H - 1 - step)]
-        if recv:
-            landed(zrecv.at[q - 1, rows, :], rs_recv.at[2 * (q - 1) + hf])
-            val = val + zrecv[q - 1, rows, :].astype(F32)
-        zsend[q, rows, :] = val.astype(BF16)
-        if step < H - 1:
-            send(
-                zsend.at[q, rows, :], zrecv.at[q, rows, :], rs_sent.at[2 * q + hf], rs_recv.at[2 * q + hf],
-                at_z(rs_z, k),
-            )
-        else:
-            send(zsend.at[q, rows, :], zfin.at[n, k], fin_sent.at[2 * n + hf], fin_recv.at[2 * n + k], at_z(rs_z, hf))
+        for m in (0, 1):
+            rows = pl.ds(mult(B * hf + HP * m, 32), HP)
+            val = grad[n, rows, lanes(H - 1 - step)]
+            if recv:
+                landed(zrecv.at[q - 1, rows, :], rs_recv.at[4 * (q - 1) + 2 * hf + m])
+                val = val + zrecv[q - 1, rows, :].astype(F32)
+            zsend[q, rows, :] = val.astype(BF16)
+            src = zsend.at[q, rows, :]
+            s = 4 * q + 2 * hf + m
+            if step < H - 1:
+                send(src, zrecv.at[q, rows, :], rs_sent.at[s], rs_recv.at[s], at_z(rs_z, k))
+            else:
+                dst = zfin.at[n, k, pl.ds(HP * m, HP), :]
+                send(src, dst, rs_sent.at[s], fin_recv.at[4 * n + 2 * k + m], at_z(rs_z, hf))
 
     def RS(n, step):
         if step == 0:
@@ -294,11 +318,12 @@
                 zsend[q] = grad[n, :, lanes(LAST)].astype(BF16)
 
             for hf, to in ((0, at_z(up, 1)), (1, at_z(down, 0))):
-                rows = pl.ds(B * hf, B)
-                send(
-                    zsend.at[q, rows, :], zrecv.at[q, rows, :], rs_sent.at[2 * q + hf], rs_recv.at[2 * q + hf], to,
-                    when=k == 1,
-                )
+                for m in (0, 1):
+                    rows = pl.ds(B * hf + HP * m, HP)
+                    s = 4 * q + 2 * hf + m
+                    send(
+                        zsend.at[q, rows, :], zrecv.at[q, rows, :], rs_sent.at[s], rs_recv.at[s], to, when=k == 1
+                    )
             rs_one(n, 1, k, False)
             send(
                 grad.at[n, pl.ds(B, B), lanes(LAST)], ownp.at[n], f_send.at[2 + n], f_recv.at[2 + n], sib, when=k == 0
@@ -311,17 +336,18 @@
 
     def RS_end(n):
         for d in (0, 1):
-            landed(zfin.at[n, d], fin_recv.at[2 * n + d])
+            for m in (0, 1):
+                landed(zfin.at[n, d, pl.ds(HP * m, HP), :], fin_recv.at[4 * n + 2 * d + m])
         tot = zfin[n, 0].astype(F32) + zfin[n, 1].astype(F32)
 
         @pl.when(k == 0)
         def _():
-            res[n] = tot + grad[n, 0:B, lanes(LAST)]
+            (outg_out, ing_out)[n][...] = tot + grad[n, 0:B, lanes(LAST)]
 
         @pl.when(k == 1)
         def _():
             landed(ownp.at[n], f_recv.at[2 + n])
-            res[n] = tot + ownp[n]
+            (outg_out, ing_out)[n][...] = tot + ownp[n]
 
     TR = min(128, RC)
 
@@ -372,131 +398,121 @@
         c.start()
     entry_wait()
     ag_start(0)
-    own_wout()
     a2a_start(tokens, tokb, 0)
-    ag_start(1)
-    a2a_start(upstream, upb, 1)
     ag(0, 0, 0)
     ag(0, 0, 1)
-    ag(1, 0, 0)
+    a2a_start(upstream, upb, 1)
     ag(0, 1, 0)
-    ag(1, 0, 1)
+    own_wout()
+    ag(0, 1, 1)
     A2F(0)
-    ag(0, 1, 1)
-    ag(1, 1, 0)
+    ag_start(1)
     A2W(0)
-    P_(0, 1, 1)
-    ag(1, 1, 1)
+    P_(0, 0, 1)
+    S_(0, 0)
     ag(0, 2, 0)
-    P_(0, 0, 1)
-    A2F(1)
-    S_(0, 1)
     ag(0, 2, 1)
     P_(0, 2, 1)
-    S_(0, 0)
-    ag(1, 2, 0)
     S_(0, 2)
-    ag(1, 2, 1)
-    A2W(1)
-    P_(1, 2, 1)
-    S_(1, 2)
+    P_(0, 1, 1)
+    S_(0, 1)
+    ag(1, 0, 0)
+    A2F(1)
+    ag(1, 0, 1)
     ag(0, 3, 1)
     ag(0, 3, 0)
     P_(0, 3, 1)
     S_(0, 3)
-    P_(1, 0, 2)
+    ag(1, 1, 0)
+    U_(0, 2)
+    A2W(1)
+    U_(0, 0)
+    P_(1, 0, 1)
+    ag(1, 1, 1)
+    S_(1, 0)
+    P_(1, 1, 1)
+    U_(0, 1)
+    transpose(w1T, w1)
+    ag(1, 2, 0)
+    U_(0, 3)
+    V_(0, 2)
+    S_(1, 1)
+    ag(1, 2, 1)
+    P_(1, 2, 1)
+    S_(1, 2)
+    V_(0, 1)
+    transpose(upT, upb)
+    V_(0, 3)
+    GV(0, 2)
+    V_(0, 0)
+    U_(1, 0)
     ag(1, 3, 0)
-    transpose(upT, upb)
-    S_(1, 0)
     ag(1, 3, 1)
     P_(1, 3, 1)
-    U_(0, 2)
     S_(1, 3)
     U_(1, 2)
-    U_(0, 3)
-    U_(0, 0)
-    S_(1, 1)
-    V_(0, 2)
-    U_(0, 1)
+    GV(0, 3)
+    GV(0, 0)
+    GU(0, 2)
+    U_(1, 1)
+    V_(1, 0)
     U_(1, 3)
-    U_(1, 0)
-    V_(0, 3)
-    V_(1, 2)
-    V_(0, 0)
-    U_(1, 1)
-    GV(0, 2)
-    V_(0, 1)
-    V_(1, 3)
-    V_(1, 0)
-    GV(0, 3)
-    GV(1, 2)
-    V_(1, 1)
-    GV(1, 3)
-    GU(0, 2)
-    transpose(tokT, tokb)
     GV(0, 1)
     grad_mm(0, 2, 1)
+    V_(1, 2)
     GU(0, 3)
     grad_mm(0, 3, 1)
     RS(0, 0)
+    V_(1, 1)
+    V_(1, 3)
+    GU(0, 1)
+    transpose(tokT, tokb)
+    GV(1, 0)
+    GV(1, 2)
+    RS(0, 1)
+    GU(0, 0)
+    GV(1, 1)
+    grad_mm(0, 1, 1)
+    GV(1, 3)
+    drain(40)
+    RS(0, 2)
     GU(1, 2)
-    GV(1, 0)
-    GV(0, 0)
-    GV(1, 1)
+    GU(1, 1)
+    GU(1, 0)
     grad_mm(1, 2, 1)
     GU(1, 3)
     grad_mm(1, 3, 1)
     RS(1, 0)
-    transpose(w1T, w1)
-    GU(0, 1)
-    GU(0, 0)
-    RS(0, 1)
-    GU(1, 0)
-    GU(1, 1)
+    grad_mm(1, 0, 2)
     TG()
     RS(1, 1)
-    grad_mm(1, 1, 1)
-    grad_mm(0, 1, 1)
-    drain(40)
-    RS(0, 2)
     grad_mm(0, 0, 1)
-    grad_mm(1, 0, 1)
+    RS(0, 3)
+    TG2()
     drain(40)
     RS(1, 2)
-    TG2()
-    RS(0, 3)
+    RS_end(0)
     drain(40)
     RS(1, 3)
-    RS_end(0)
-    c_o = pltpu.make_async_copy(res.at[0], outg_out, loc_sem.at[0])
-    c_o.start()
     TGE()
     RS_end(1)
-    c_i = pltpu.make_async_copy(res.at[1], ing_out, loc_sem.at[2])
-    c_i.start()
     drain()
     for n in range(3):
         a2a_wait(n, a2a_send)
-    c_o.wait()
-    c_i.wait()
-
-
-def finish(tg, ing, outg, tg_o, ing_o, outg_o, tb, tf, sem):
+
+
+def finish(tg, ing, outg, tg_o, ing_o, outg_o, tf, sem):
     NC = 4
-    D = tb.shape[1]
+    D = tg.shape[1]
     C = D // NC
     c_o = pltpu.make_async_copy(outg, outg_o, sem.at[0])
     c_o.start()
     c_i = pltpu.make_async_copy(ing, ing_o, sem.at[1])
     c_i.start()
-    ins = [pltpu.make_async_copy(tg.at[:, pl.ds(C * c, C)], tb.at[:, pl.ds(C * c, C)], sem.at[2 + c]) for c in range(NC)]
-    for c in ins:
-        c.start()
     outs = []
     for n in range(NC):
-        ins[n].wait()
         cols = pl.ds(C * n, C)
-        tf[:, cols] = tb[:, cols].astype(F32)
+        tf[:, cols] = tg[:, cols].astype(F32)
         o = pltpu.make_async_copy(tf.at[:, cols], tg_o.at[:, cols], sem.at[2 + NC + n])
         o.start()
         outs.append(o)
@@ -541,7 +557,9 @@
             VM((2, NS - 1, UR, HL), F32),
             VM((2, UR, HL), F32),
             VM((2, NS - 1, VR, HL), F32),
+            VM((2, NS, UR, 128), F32),
             VM((VR, HL), F32),
+            VM((UR, 128), F32),
             VM((2, R, HL), BF16),
             VM((2, BC, HL), F32),
             VM((2, B, 128), F32),
@@ -551,7 +569,6 @@
             VM((R, BC), F32),
             VM((RC, BC), F32),
             VM((RC, BC), BF16),
-            VM((2, B, 128), F32),
             DMA((5,)),
             DMA((3,)),
             DMA((3,)),
@@ -559,10 +576,9 @@
             DMA((5,)),
             DMA((8 * H,)),
             DMA((8 * H,)),
-            DMA((4 * H,)),
-            DMA((4 * H,)),
-            DMA((4,)),
-            DMA((4,)),
+            DMA((8 * H,)),
+            DMA((8 * H,)),
+            DMA((8,)),
             DMA((4 * H, NS - 1)),
             DMA((4 * H, NS - 1)),
             DMA((4 * H, NS - 1)),
@@ -576,7 +592,11 @@
                 jax.ShapeDtypeStruct((B, 128), F32),
             ),
             in_specs=[pl.BlockSpec(memory_space=pl.ANY)] * 4,
-            out_specs=tuple([pl.BlockSpec(memory_space=pl.ANY)] * 3),
+            out_specs=(
+                pl.BlockSpec(memory_space=pl.ANY),
+                pl.BlockSpec(memory_space=pltpu.VMEM),
+                pl.BlockSpec(memory_space=pltpu.VMEM),
+            ),
             scratch_shapes=scratch,
             compiler_params=pltpu.CompilerParams(
                 collective_id=0, has_side_effects=True, vmem_limit_bytes=105 * 2**19
@@ -589,10 +609,9 @@
                 jax.ShapeDtypeStruct((B, 128), F32),
                 jax.ShapeDtypeStruct((B, 128), F32),
             ),
-            in_specs=[pl.BlockSpec(memory_space=pl.ANY)] * 3,
+            in_specs=[pl.BlockSpec(memory_space=pltpu.VMEM)] * 3,
             out_specs=tuple([pl.BlockSpec(memory_space=pl.ANY)] * 3),
             scratch_shapes=[
-                pltpu.VMEM((T, D), BF16),
                 pltpu.VMEM((T, D), F32),
                 DMA((10,)),
             ],

time: 81.2 us -> 80 us (0.985)
  Pallas kernels: 80.4 us -> 79.3 us
    pallas_call x1, Pallas kernels: 78.9 us -> 78 us  [per_device(): pl.pallas_call(functools.partial(kernel, cfg), out_shape=(jax.ShapeDtypeS...]
where the time goes in v5:
time: 80 us
  Pallas kernels  79.3 us (99%)
    pallas_call x1, Pallas kernels, per_device(): pl.pallas_call(functools.partial(kernel, cfg), out_shape=(jax.ShapeDtypeS...  78 us

profile of v5, /device:TPU:1, one launch (start us, length us, event | category | flops | bytes accessed | tf_op | source)
XLA Modules:
  0.0 80.0 jit_solution(5830691593683973148)
XLA Ops:
  0.6 78.0 %shard_map.67 = (bf16[16,18432]{1,0:T(8,128)(2,1)S(1)}, f32[576,128]{1,0:T(8,128)S(1)}, f32[576,128]{1,0:T(8,128)S(1)}) custom-call(bf16[16,18432]{1,0:T(8,128)(2,1)} %tokens.1, bf16[16,18432]{1,0:T(8,128)(2,1)} %upstream.1, bf16[18432,128]{1,0:T(8,128)(2,1)} %w_in.1, bf16[128,18432]{1,0:T(8,128)(2,1)} %w_out.1), custom_call_target="tpu_custom_call" | custom-call | tf_op jit(solution)/shard_map/pallas_call | solution.py:587
  78.7 1.3 %shard_map.68 = (f32[16,18432]{1,0:T(8,128)}, f32[576,128]{1,0:T(8,128)}, f32[576,128]{1,0:T(8,128)}) custom-call(bf16[16,18432]{1,0:T(8,128)(2,1)S(1)} %get-tuple-element.9.tg, f32[576,128]{1,0:T(8,128)S(1)} %get-tuple-element.10.ing, f32[576,128]{1,0:T(8,128)S(1)} %get-tuple-element.11.outg), custom_call_target="tpu_custom_call" | custom-call | tf_op jit(solution)/shard_map/pallas_call | solution.py:605

commit v6 on v5

--- a/solution.py
+++ b/solution.py
@@ -491,9 +491,9 @@
     TG2()
     drain(40)
     RS(1, 2)
-    RS_end(0)
     drain(40)
     RS(1, 3)
+    RS_end(0)
     TGE()
     RS_end(1)
     drain()

time: 80 us -> 79.7 us (level)
  no operation moved by 1% of the time
where the time goes in v6:
time: 79.7 us
  Pallas kernels  79 us (99%)
    pallas_call x1, Pallas kernels, per_device(): pl.pallas_call(functools.partial(kernel, cfg), out_shape=(jax.ShapeDtypeS...  77.7 us

profile of v6, /device:TPU:1, one launch (start us, length us, event | category | flops | bytes accessed | tf_op | source)
XLA Modules:
  0.0 79.7 jit_solution(7766941229340699951)
XLA Ops:
  0.6 77.7 %shard_map.67 = (bf16[16,18432]{1,0:T(8,128)(2,1)S(1)}, f32[576,128]{1,0:T(8,128)S(1)}, f32[576,128]{1,0:T(8,128)S(1)}) custom-call(bf16[16,18432]{1,0:T(8,128)(2,1)} %tokens.1, bf16[16,18432]{1,0:T(8,128)(2,1)} %upstream.1, bf16[18432,128]{1,0:T(8,128)(2,1)} %w_in.1, bf16[128,18432]{1,0:T(8,128)(2,1)} %w_out.1), custom_call_target="tpu_custom_call" | custom-call | tf_op jit(solution)/shard_map/pallas_call | solution.py:587
  78.4 1.3 %shard_map.68 = (f32[16,18432]{1,0:T(8,128)}, f32[576,128]{1,0:T(8,128)}, f32[576,128]{1,0:T(8,128)}) custom-call(bf16[16,18432]{1,0:T(8,128)(2,1)S(1)} %get-tuple-element.9.tg, f32[576,128]{1,0:T(8,128)S(1)} %get-tuple-element.10.ing, f32[576,128]{1,0:T(8,128)S(1)} %get-tuple-element.11.outg), custom_call_target="tpu_custom_call" | custom-call | tf_op jit(solution)/shard_map/pallas_call | solution.py:605

commit v7 on v6

--- a/solution.py
+++ b/solution.py
@@ -475,11 +475,12 @@
     grad_mm(0, 1, 1)
     GV(1, 3)
     drain(40)
-    RS(0, 2)
+    rs_one(0, 2, k, True)
     GU(1, 2)
+    grad_mm(1, 2, 1)
+    rs_one(0, 2, 1 - k, True)
     GU(1, 1)
     GU(1, 0)
-    grad_mm(1, 2, 1)
     GU(1, 3)
     grad_mm(1, 3, 1)
     RS(1, 0)

time: 79.7 us -> 79.7 us (level)
  no operation moved by 1% of the time
where the time goes in v7:
time: 79.7 us
  Pallas kernels  79 us (99%)
    pallas_call x1, Pallas kernels, per_device(): pl.pallas_call(functools.partial(kernel, cfg), out_shape=(jax.ShapeDtypeS...  77.7 us

profile of v7, /device:TPU:1, one launch (start us, length us, event | category | flops | bytes accessed | tf_op | source)
XLA Modules:
  0.0 79.7 jit_solution(3973678244621604348)
XLA Ops:
  0.6 77.7 %shard_map.67 = (bf16[16,18432]{1,0:T(8,128)(2,1)S(1)}, f32[576,128]{1,0:T(8,128)S(1)}, f32[576,128]{1,0:T(8,128)S(1)}) custom-call(bf16[16,18432]{1,0:T(8,128)(2,1)} %tokens.1, bf16[16,18432]{1,0:T(8,128)(2,1)} %upstream.1, bf16[18432,128]{1,0:T(8,128)(2,1)} %w_in.1, bf16[128,18432]{1,0:T(8,128)(2,1)} %w_out.1), custom_call_target="tpu_custom_call" | custom-call | tf_op jit(solution)/shard_map/pallas_call | solution.py:588
  78.4 1.3 %shard_map.68 = (f32[16,18432]{1,0:T(8,128)}, f32[576,128]{1,0:T(8,128)}, f32[576,128]{1,0:T(8,128)}) custom-call(bf16[16,18432]{1,0:T(8,128)(2,1)S(1)} %get-tuple-element.9.tg, f32[576,128]{1,0:T(8,128)S(1)} %get-tuple-element.10.ing, f32[576,128]{1,0:T(8,128)S(1)} %get-tuple-element.11.outg), custom_call_target="tpu_custom_call" | custom-call | tf_op jit(solution)/shard_map/pallas_call | solution.py:606
